TPU v7x, 256 devices: a whole 4x4x8 slice. The times are simulated.
256 devices in a mesh: section: 2 (over core), expert: 128 (over x, y, z).
Axes of the slice: x: 4, y: 4, z: 8, core: 2. Of those that a mesh axis runs over, the one named last changes fastest.
Arguments:
- hidden: bfloat16 [2, 16384, 2048], P('section', 'expert'), may hold values from -6 to 6
- routes: int32 [2, 16384, 2], P('section', 'expert'), may hold values from 0 to 127, all different within a row; in each aligned block of 128 rows (0 to 127, 128 to 255, ..., all dimensions but the last counted through in order) at most 4 rows name the same one
- gates: float32 [2, 16384, 2], P('section', 'expert'), may hold values from 0.2 to 1
- lengths: int32 [2, 128], P('section', 'expert'), may hold values from 64 to 128, as said below
- w_in: bfloat16 [2, 2048, 131072], P('section', None, 'expert'), may hold values from -0.125 to 0.125
- w_out: bfloat16 [2, 131072, 2048], P('section', 'expert'), may hold values from -0.0625 to 0.0625
- incoming: bfloat16 [2, 16384, 2048], P(None, 'expert', 'section'), may hold values from -6 to 6
Outputs:
- outputs: bfloat16 [2, 16384, 2048], P('section', 'expert')
- hidden_grad: bfloat16 [2, 16384, 2048], P('section', 'expert')
- gate_grad: float32 [2, 16384, 2], P('section', 'expert')
Inputs may be any that keep to these rules, and one draw needn't show every extreme that they name: `routes`: each row names two different experts. Among the rows of one sentence no expert is named more than 4 times, a bound that some block reaches. `lengths`: each layer has a sentence of exactly 128 tokens.
All inputs are finite; a program needn't handle non-finite values.
Results may differ from a plain program's by a relative error of at most 0.013.
Values may be sent and summed in bfloat16 or wider, within the bound.
No kernel may reach another device: no remote copies, remote signals or barrier semaphores. Data moves between devices by JAX's collectives and lax.ppermute only.
A program may use at most 64 MiB of HBM per device.

v0:
```python
import functools

import jax
import jax.numpy as jnp
from jax import lax
from jax.experimental import pallas as pl
from jax.experimental.pallas import tpu as pltpu
from jax.sharding import PartitionSpec as P

SPLIT = 8
CAP = 4
LIVE = 16
SLOTS = LIVE * CAP
EPS = 1e-05
COST = 32
BF = jnp.bfloat16
F32 = jnp.float32
VMEM_LIMIT = 16 * 2**20


def hop(value, step):
    n = lax.axis_size("expert")
    pairs = [(i, i // SPLIT * SPLIT + (i + step) % SPLIT) for i in range(n)]
    return lax.ppermute(value, "expert", pairs)


def swap_plane(rows):
    n = lax.axis_size("expert")
    groups = [[c * SPLIT + p for c in range(n // SPLIT)] for p in range(SPLIT)]
    count, width = rows.shape
    lanes = 128
    packed = rows.reshape(n // SPLIT, count * SPLIT // n * width // lanes, lanes)
    moved = lax.all_to_all(
        packed, "expert", split_axis=0, concat_axis=0, axis_index_groups=groups, tiled=True
    )
    return moved.reshape(count, width)


def swap_pair(rows):
    n = lax.axis_size("expert")
    half = SPLIT // 2
    groups = [[c * SPLIT + q for q in (p, p + half) for c in range(n // SPLIT)] for p in range(half)]
    count, width = rows.shape
    lanes = 128
    packed = rows.reshape(len(groups[0]), count * width // lanes // len(groups[0]), lanes)
    moved = lax.all_to_all(
        packed, "expert", split_axis=0, concat_axis=0, axis_index_groups=groups, tiled=True
    )
    return moved.reshape(count, width)


def nearer(pair, flip):
    half = pair.shape[0] // 2
    return jnp.where(flip, pair[half:], pair[:half])


def exchange(rows, flips, expert):
    pair = swap_pair(rows)
    up, down = hop(pair, 1), hop(pair, -1)
    ((own, across),) = expert(0, [pair])
    sum_up = hop(across, 1)
    up_2, down_2 = hop(nearer(up, flips[1] == 1), 1), hop(nearer(down, flips[2] == 1), -1)
    (low_1, high_3), (high_1, low_3) = expert(1, [up, down])
    sum_up, sum_down = hop(plus(sum_up, high_3), 1), hop(low_3, -1)
    low_2, high_2 = expert(2, [up_2, down_2])
    sum_up, sum_down = hop(plus(sum_up, high_2), 1), hop(plus(sum_down, low_2), -1)
    sum_up, sum_down = hop(plus(sum_up, high_1), 1), hop(plus(sum_down, low_1), -1)
    return (own.astype(F32) + sum_up.astype(F32) + sum_down.astype(F32)).astype(BF)


def plus(a, b):
    return (a.astype(F32) + b.astype(F32)).astype(BF)


def normalize(values):
    center = values - jnp.mean(values, axis=-1, keepdims=True)
    scale = lax.rsqrt(jnp.mean(center * center, axis=-1, keepdims=True) + EPS)
    return center * scale, scale


def norm_back(normed, scale, upstream):
    first = jnp.mean(upstream, axis=-1, keepdims=True)
    second = jnp.mean(upstream * normed, axis=-1, keepdims=True)
    return scale * (upstream - first - normed * second)


def rows_dot(a, b):
    return lax.dot_general(a, b, (((0,), (0,)), ((), ())), preferred_element_type=F32)


def column(row):
    return jnp.broadcast_to(row, (row.shape[1], row.shape[1])).T[:, 0:1]


def row(column):
    return jnp.broadcast_to(column, (column.shape[0], column.shape[0])).T[0:1, :]


def dispatch_kernel(length_ref, section_ref, routes_ref, hidden_ref, rows_ref, first_ref, second_ref):
    count = hidden_ref.shape[0]
    slot = lax.broadcasted_iota(jnp.int32, (SLOTS, count), 0)
    token = lax.broadcasted_iota(jnp.int32, (SLOTS, count), 1)
    expert, place = slot // CAP, slot % CAP
    alive = token < length_ref[0, 0]
    hit0 = alive & (routes_ref[0:1, :] == expert)
    hit1 = alive & (routes_ref[1:2, :] == expert)
    hits = jnp.where(hit0 | hit1, 1.0, 0.0).astype(BF)
    earlier = lax.broadcasted_iota(jnp.int32, (count, count), 0) < lax.broadcasted_iota(
        jnp.int32, (count, count), 1
    )
    rank = jnp.dot(hits, jnp.where(earlier, 1.0, 0.0).astype(BF), preferred_element_type=F32)
    here = rank == place.astype(F32)
    first = jnp.where(hit0 & here, 1.0, 0.0).astype(BF)
    second = jnp.where(hit1 & here, 1.0, 0.0).astype(BF)
    first_ref[...] = first
    second_ref[...] = second
    normed, _ = normalize(hidden_ref[...].astype(F32))
    rows = jnp.dot(first + second, normed.astype(BF), preferred_element_type=F32).astype(BF)
    rows_ref[:SLOTS] = rows
    rows_ref[SLOTS:] = rows


def middle_kernel(
    length_ref,
    section_ref,
    hidden_ref,
    gates_ref,
    first_ref,
    second_ref,
    y_ref,
    keep_ref,
    other_ref,
    result_ref,
    upstream_ref,
    gate_grad_ref,
    rows_ref,
):
    count = hidden_ref.shape[0]
    encoder = section_ref[0] == 0
    alive = lax.broadcasted_iota(jnp.int32, (count, 1), 0) < length_ref[0, 0]
    g0, g1 = column(gates_ref[0:1, :]), column(gates_ref[1:2, :])
    y = y_ref[...]
    y0 = rows_dot(first_ref[...], y)
    y1 = rows_dot(second_ref[...], y)
    layer_out = (hidden_ref[...].astype(F32) + g0 * y0 + g1 * y1).astype(BF)
    hat, scale = normalize(layer_out.astype(F32))
    result_ref[...] = jnp.where(encoder, hat.astype(BF), layer_out)
    keep, other = keep_ref[...].astype(F32), other_ref[...].astype(F32)
    cot = jnp.concatenate(
        [jnp.where(encoder, keep, other), jnp.where(encoder, other, keep)], axis=1
    )
    cot = jnp.where(alive, cot, 0.0)
    upstream = jnp.where(encoder, norm_back(hat, scale, cot), cot).astype(BF)
    upstream_ref[...] = upstream
    up32 = upstream.astype(F32)
    gate_grad_ref[0:1, :] = row(jnp.sum(up32 * y0, axis=-1, keepdims=True))
    gate_grad_ref[1:2, :] = row(jnp.sum(up32 * y1, axis=-1, keepdims=True))
    rows = jnp.dot(first_ref[...], (g0 * up32).astype(BF), preferred_element_type=F32)
    rows += jnp.dot(second_ref[...], (g1 * up32).astype(BF), preferred_element_type=F32)
    rows_ref[:SLOTS] = rows.astype(BF)
    rows_ref[SLOTS:] = rows.astype(BF)


def final_kernel(hidden_ref, upstream_ref, first_ref, second_ref, d_ref, out_ref):
    normed, scale = normalize(hidden_ref[...].astype(F32))
    d_normed = rows_dot(first_ref[...] + second_ref[...], d_ref[...])
    out_ref[...] = (upstream_ref[...].astype(F32) + norm_back(normed, scale, d_normed)).astype(BF)


def stack(refs):
    return jnp.concatenate([ref[...] for ref in refs], axis=0) if len(refs) > 1 else refs[0][...]


def spread(refs, terms, flip_ref, start):
    rows = refs[0].shape[0]
    for i in range(0, len(refs), 1 if start is None else 2):
        part = terms[i * rows : (i + 1) * rows]
        if start is None:
            refs[i][...] = part.astype(BF)
            continue
        other = terms[(i + 1) * rows : (i + 2) * rows]
        flip = flip_ref[start + i // 2] == 1
        refs[i][...] = jnp.where(flip, other, part).astype(BF)
        refs[i + 1][...] = jnp.where(flip, part, other).astype(BF)


def forward_kernel(count, start, flip_ref, *refs):
    blocks, (w_in_ref, w_out_ref) = refs[:count], refs[count : count + 2]
    act_ref, parts = refs[count + 2], refs[count + 3 :]
    act = jnp.dot(stack(blocks), w_in_ref[...], preferred_element_type=F32)
    act = jnp.maximum(act, 0.0).astype(BF)
    act_ref[...] = act
    spread(parts, jnp.dot(act, w_out_ref[...], preferred_element_type=F32), flip_ref, start)


def backward_kernel(count, start, flip_ref, *refs):
    blocks, (act_ref, w_in_t_ref, w_out_t_ref) = refs[:count], refs[count : count + 3]
    d_act = jnp.dot(stack(blocks), w_out_t_ref[...], preferred_element_type=F32)
    d_pre = jnp.where(act_ref[...] > 0, d_act, 0.0).astype(BF)
    terms = jnp.dot(d_pre, w_in_t_ref[...], preferred_element_type=F32)
    spread(refs[count + 3 :], terms, flip_ref, start)


def turn_kernel(w_in_ref, w_out_ref, w_in_t_ref, w_out_t_ref):
    w_in_t_ref[...] = w_in_ref[...].T
    w_out_t_ref[...] = w_out_ref[...].T


def call(kernel, outs, scalars, *arrays, flops=0, limit=VMEM_LIMIT):
    vmem = pl.BlockSpec(memory_space=pltpu.VMEM)
    return pl.pallas_call(
        kernel,
        out_shape=outs,
        in_specs=[pl.BlockSpec(memory_space=pltpu.SMEM)] * scalars + [vmem] * (len(arrays) - scalars),
        out_specs=jax.tree.map(lambda _: vmem, outs),
        compiler_params=pltpu.CompilerParams(vmem_limit_bytes=limit),
        cost_estimate=pl.CostEstimate(flops=flops, bytes_accessed=2**20, transcendentals=0),
    )(*arrays)


def per_device(hidden, routes, gates, lengths, w_in, w_out, incoming):
    section = lax.axis_index("section")
    source, w_in, w_out = hidden[0], w_in[0], w_out[0]
    count, width = source.shape
    wide = jax.ShapeDtypeStruct((count, width), BF)
    slots = jax.ShapeDtypeStruct((SLOTS, width), BF)
    twice = jax.ShapeDtypeStruct((2 * SLOTS, width), BF)
    table = jax.ShapeDtypeStruct((SLOTS, count), BF)
    section_id = jnp.reshape(section.astype(jnp.int32), (1,))

    keep = jnp.where(section == 0, incoming[0], incoming[1])
    send = jnp.where(section == 0, incoming[1], incoming[0])
    other = lax.ppermute(send, "section", [(0, 1), (1, 0)])

    rows, first, second = call(
        dispatch_kernel, [twice, table, table], 2, lengths, section_id, routes[0].T, source
    )

    turned = [jax.ShapeDtypeStruct(w.shape[::-1], BF) for w in (w_in, w_out)]
    w_in_t, w_out_t = call(turn_kernel, turned, 0, w_in, w_out, limit=32 * 2**20)
    hidden_units = w_in.shape[1]
    plane = lax.axis_index("expert") % SPLIT
    flips = jnp.stack([(plane + d) % SPLIT // (SPLIT // 2) for d in (0, -1, 1)]).astype(jnp.int32)
    acts = {}

    def run(kernel, key, blocks, extra, outs):
        start = (0, 1, None)[key]
        total = sum(b.shape[0] for b in blocks)
        outs = outs + [slots] * (total // SLOTS)
        got = call(
            functools.partial(kernel, len(blocks), start),
            outs,
            1,
            flips,
            *blocks,
            *extra,
            flops=COST * total * width * hidden_units,
        )
        terms = got[len(outs) - total // SLOTS :]
        return got, terms if start is None else list(zip(terms[::2], terms[1::2]))

    def forward(key, blocks):
        total = sum(b.shape[0] for b in blocks)
        outs = [jax.ShapeDtypeStruct((total, hidden_units), BF)]
        got, terms = run(forward_kernel, key, blocks, [w_in, w_out], outs)
        acts[key] = got[0]
        return terms

    def backward(key, blocks):
        return run(backward_kernel, key, blocks, [acts[key], w_in_t, w_out_t], [])[1]

    y = swap_plane(exchange(rows, flips, forward))

    result, upstream, gate_grad, grad_rows = call(
        middle_kernel,
        [wide, wide, jax.ShapeDtypeStruct((2, count), F32), twice],
        2,
        lengths,
        section_id,
        source,
        gates[0].T,
        first,
        second,
        y,
        keep,
        other,
    )

    d_rows = swap_plane(exchange(grad_rows, flips, backward))

    hidden_grad = call(final_kernel, wide, 0, source, upstream, first, second, d_rows)
    return (result[None], hidden_grad[None], gate_grad.T[None])


def solution(mesh):
    in_specs = (
        P("section", "expert", None),
        P("section", "expert", None),
        P("section", "expert", None),
        P("section", "expert"),
        P("section", None, "expert"),
        P("section", "expert", None),
        P(None, "expert", "section"),
    )
    out_specs = (
        P("section", "expert", None),
        P("section", "expert", None),
        P("section", "expert", None),
    )
    return jax.shard_map(
        per_device, mesh=mesh, in_specs=in_specs, out_specs=out_specs, check_vma=False
    )
```

profile of v0, /device:TPU:8, one launch (start us, length us, event | category | flops | bytes accessed | tf_op | source)
XLA Modules:
  0.0 186.2 jit_solution(17360779163149136135)
XLA Ops:
  4.6 14.2 %all-to-all-start = ((bf16[32,64,128]{2,1,0:T(8,128)(2,1)}), bf16[32,64,128]{2,1,0:T(8,128)(2,1)S(1)}, u32[]{:S(2)}, u32[]{:S(2)}) async-start(bf16[32,64,128]{2,1,0:T(8,128)(2,1)} %reshape.38), calls=%async_computation | async-start | bytes 1048576 | tf_op jit(solution)/shard_map/all_to_all | solution.py:46
  19.0 15.2 %all-to-all-done = bf16[32,64,128]{2,1,0:T(8,128)(2,1)S(1)} async-done(((bf16[32,64,128]{2,1,0:T(8,128)(2,1)}), bf16[32,64,128]{2,1,0:T(8,128)(2,1)S(1)}, u32[]{:S(2)}, u32[]{:S(2)}) %all-to-all-start) | async-done | bytes 524320 | tf_op jit(solution)/shard_map/all_to_all | solution.py:46
  34.4 5.5 %collective-permute-start.1 = (bf16[128,2048]{1,0:T(8,128)(2,1)S(1)}, bf16[128,2048]{1,0:T(8,128)(2,1)S(1)}, u32[]{:S(2)}, u32[]{:S(2)}) collective-permute-start(bf16[128,2048]{1,0:T(8,128)(2,1)S(1)} %reshape.39.refs_0_), channel_id=1, source_target_pairs={{0,1},{1,2},{2,3},{3,4},{4,5},{5,6},{6,7},{7,0},{8,9},{9,10},{10,1... | collective-permute-start | bytes 1572872 | tf_op jit(solution)/shard_map/ppermute | solution.py:24
  39.9 2.2 %copy-done.2 = bf16[1,2048,1024]{2,1,0:T(8,128)(2,1)S(1)} copy-done((bf16[1,2048,1024]{2,1,0:T(8,128)(2,1)S(1)}, bf16[1,2048,1024]{2,1,0:T(8,128)(2,1)}, u32[]{:S(2)}) %copy-start.2) | copy-done | bytes 4194328
  42.1 2.2 %copy-done.5 = bf16[1,1024,2048]{2,1,0:T(8,128)(2,1)S(1)} copy-done((bf16[1,1024,2048]{2,1,0:T(8,128)(2,1)S(1)}, bf16[1,1024,2048]{2,1,0:T(8,128)(2,1)}, u32[]{:S(2)}) %copy-start.5) | copy-done | bytes 4194328
  44.3 1.9 %shard_map.95 = (bf16[128,1024]{1,0:T(8,128)(2,1)S(1)}, bf16[64,2048]{1,0:T(8,128)(2,1)S(1)}, bf16[64,2048]{1,0:T(8,128)(2,1)S(1)}) custom-call(s32[3]{0:T(128)S(1)} %pad_add_fusion.flip_ref, bf16[128,2048]{1,0:T(8,128)(2,1)S(1)} %reshape.39.refs_0_, bf16[2048,1024]{1,0:T(8,128)(2,1)S(1)} %bitcast.25, bf16[1024,2048]{1,0:T(8,128)(2,1)S(1)} %bitcast.29), custom_call_target="tpu_custom_call" | custom-call | flops 8589934592 | bytes 1048576 | tf_op jit(solution)/shard_map/pallas_call | solution.py:211
  46.2 2.1 %collective-permute-start = (bf16[64,2048]{1,0:T(8,128)(2,1)S(1)}, bf16[64,2048]{1,0:T(8,128)(2,1)S(1)}, u32[]{:S(2)}, u32[]{:S(2)}) collective-permute-start(bf16[64,2048]{1,0:T(8,128)(2,1)S(1)} %get-tuple-element.35), channel_id=1, source_target_pairs={{0,1},{1,2},{2,3},{3,4},{4,5},{5,6},{6,7},{7,0},{8,9},{9,10},{10,1... | collective-permute-start | bytes 786440 | tf_op jit(solution)/shard_map/ppermute | solution.py:24
  48.3 4.0 %collective-permute-done.1.refs_0_ = bf16[128,2048]{1,0:T(8,128)(2,1)S(1)} collective-permute-done((bf16[128,2048]{1,0:T(8,128)(2,1)S(1)}, bf16[128,2048]{1,0:T(8,128)(2,1)S(1)}, u32[]{:S(2)}, u32[]{:S(2)}) %collective-permute-start.1) | collective-permute-done | bytes 524320 | tf_op jit(solution)/shard_map/ppermute | solution.py:24
  52.3 2.6 %collective-permute-start.4 = (bf16[64,2048]{1,0:T(8,128)(2,1)S(1)}, bf16[64,2048]{1,0:T(8,128)(2,1)S(1)}, u32[]{:S(2)}, u32[]{:S(2)}) collective-permute-start(bf16[64,2048]{1,0:T(8,128)(2,1)S(1)} %slice_select_fusion.3), channel_id=1, source_target_pairs={{0,1},{1,2},{2,3},{3,4},{4,5},{5,6},{6,7},{7,0},{8,9},{9,10},{10,1... | collective-permute-start | bytes 786440 | tf_op jit(solution)/shard_map/ppermute | solution.py:24
  55.8 2.9 %shard_map.96 = (bf16[256,1024]{1,0:T(8,128)(2,1)S(1)}, bf16[64,2048]{1,0:T(8,128)(2,1)S(1)}, bf16[64,2048]{1,0:T(8,128)(2,1)S(1)}, bf16[64,2048]{1,0:T(8,128)(2,1)S(1)}, bf16[64,2048]{1,0:T(8,128)(2,1)S(1)}) custom-call(s32[3]{0:T(128)S(1)} %pad_add_fusion.flip_ref, bf16[128,2048]{1,0:T(8,128)(2,1)S(1)} %collective-permute-done.1.refs_0_, ...), custom_call_target="tpu_custom_call" | custom-call | flops 17179869184 | bytes 1048576 | tf_op jit(solution)/shard_map/pallas_call | solution.py:211
  58.7 1.8 collective-permute-start.3
  60.5 1.5 collective-permute-start.8
  62.0 1.5 collective-permute-done.4.refs_0_
  64.0 1.9 %shard_map.97 = (bf16[128,1024]{1,0:T(8,128)(2,1)S(1)}, bf16[64,2048]{1,0:T(8,128)(2,1)S(1)}, bf16[64,2048]{1,0:T(8,128)(2,1)S(1)}) custom-call(s32[3]{0:T(128)S(1)} %pad_add_fusion.flip_ref, bf16[64,2048]{1,0:T(8,128)(2,1)S(1)} %collective-permute-done.4.refs_0_, bf16[64,2048]{1,0:T(8,128)(2,1)S(1)} %collective-permute-done.5.refs_1_, ...), custom_call_target="tpu_custom_call" | custom-call | flops 8589934592 | bytes 1048576 | tf_op jit(solution)/shard_map/pallas_call | solution.py:211
  66.9 2.7 %collective-permute-start.6 = (bf16[64,2048]{1,0:T(8,128)(2,1)S(1)}, bf16[64,2048]{1,0:T(8,128)(2,1)S(1)}, u32[]{:S(2)}, u32[]{:S(2)}) collective-permute-start(bf16[64,2048]{1,0:T(8,128)(2,1)S(1)} %add_convert_fusion.10), channel_id=1, source_target_pairs={{0,1},{1,2},{2,3},{3,4},{4,5},{5,6},{6,7},{7,0},{8,9},{9,10},{10,1... | collective-permute-start | bytes 786440 | tf_op jit(solution)/shard_map/ppermute | solution.py:24
  70.6 4.2 %collective-permute-done.6 = bf16[64,2048]{1,0:T(8,128)(2,1)S(1)} collective-permute-done((bf16[64,2048]{1,0:T(8,128)(2,1)S(1)}, bf16[64,2048]{1,0:T(8,128)(2,1)S(1)}, u32[]{:S(2)}, u32[]{:S(2)}) %collective-permute-start.6) | collective-permute-done | bytes 262176 | tf_op jit(solution)/shard_map/ppermute | solution.py:24
  74.9 1.9 collective-permute-start.7
  76.8 1.5 collective-permute-start.10
  79.1 3.6 %collective-permute-done.7 = bf16[64,2048]{1,0:T(8,128)(2,1)} collective-permute-done((bf16[64,2048]{1,0:T(8,128)(2,1)S(1)}, bf16[64,2048]{1,0:T(8,128)(2,1)}, u32[]{:S(2)}, u32[]{:S(2)}) %collective-permute-start.7) | collective-permute-done | bytes 262176 | tf_op jit(solution)/shard_map/ppermute | solution.py:24
  83.9 1.1 add_convert_fusion.6
  85.2 11.9 %all_to_all.20 = bf16[16,64,128]{2,1,0:T(8,128)(2,1)S(1)} all-to-all(bf16[16,64,128]{2,1,0:T(8,128)(2,1)S(1)} %reshape.40), channel_id=1, replica_groups={{0,8,16,24,32,40,48,56,64,72,80,88,96,104,112,120},{1,9,17,25,33,41,49,..., dimensions={0} | all-to-all | bytes 524288 | tf_op jit(solution)/shard_map/all_to_all | solution.py:33
  97.2 2.5 %shard_map.98 = (bf16[128,2048]{1,0:T(8,128)(2,1)}, bf16[128,2048]{1,0:T(8,128)(2,1)S(1)}, f32[2,128]{1,0:T(2,128)}, bf16[128,2048]{1,0:T(8,128)(2,1)S(1)}) custom-call(s32[1,1]{1,0:T(1,128)S(6)} %copy.10.length_ref, s32[1]{0:T(128)} %bitcast.section_ref, bf16[128,2048]{1,0:T(8,128)(2,1)S(1)} %bitcast.23, f32[2,128]{1,0:T(2,128)S(1)} %bitcast.34, ...), custom_call_target="tpu_custom_call" | custom-call | bytes 1048576 | tf_op jit(solution)/shard_map/pallas_call | solution.py:211
  100.8 6.0 %all-to-all-start.2 = ((bf16[32,64,128]{2,1,0:T(8,128)(2,1)}), bf16[32,64,128]{2,1,0:T(8,128)(2,1)S(1)}, u32[]{:S(2)}, u32[]{:S(2)}) async-start(bf16[32,64,128]{2,1,0:T(8,128)(2,1)} %reshape.42), calls=%async_computation.2 | async-start | bytes 1048576 | tf_op jit(solution)/shard_map/all_to_all | solution.py:46
  106.8 2.2 %copy-done.4 = bf16[1,2048,1024]{2,1,0:T(8,128)(2,1)S(1)} copy-done((bf16[1,2048,1024]{2,1,0:T(8,128)(2,1)S(1)}, bf16[1,2048,1024]{2,1,0:T(8,128)(2,1)}, u32[]{:S(2)}) %copy-start.4) | copy-done | bytes 4194328
  109.0 2.2 %copy-done.6 = bf16[1,1024,2048]{2,1,0:T(8,128)(2,1)S(1)} copy-done((bf16[1,1024,2048]{2,1,0:T(8,128)(2,1)S(1)}, bf16[1,1024,2048]{2,1,0:T(8,128)(2,1)}, u32[]{:S(2)}) %copy-start.6) | copy-done | bytes 4194328
  111.2 2.4 %shard_map.99 = (bf16[1024,2048]{1,0:T(8,128)(2,1)S(1)}, bf16[2048,1024]{1,0:T(8,128)(2,1)S(1)}) custom-call(bf16[2048,1024]{1,0:T(8,128)(2,1)S(1)} %bitcast.28, bf16[1024,2048]{1,0:T(8,128)(2,1)S(1)} %bitcast.32), custom_call_target="tpu_custom_call" | custom-call | bytes 1048576 | tf_op jit(solution)/shard_map/pallas_call | solution.py:211
  113.6 2.0 %copy-done.9 = bf16[1024,2048]{1,0:T(8,128)(2,1)} copy-done((bf16[1024,2048]{1,0:T(8,128)(2,1)}, bf16[1024,2048]{1,0:T(8,128)(2,1)S(1)}, u32[]{:S(2)}) %copy-start.9) | copy-done | bytes 4194328
  115.6 2.0 %copy-done.12 = bf16[2048,1024]{1,0:T(8,128)(2,1)} copy-done((bf16[2048,1024]{1,0:T(8,128)(2,1)}, bf16[2048,1024]{1,0:T(8,128)(2,1)S(1)}, u32[]{:S(2)}) %copy-start.12) | copy-done | bytes 4194328
  117.6 3.1 %all-to-all-done.2 = bf16[32,64,128]{2,1,0:T(8,128)(2,1)S(1)} async-done(((bf16[32,64,128]{2,1,0:T(8,128)(2,1)}), bf16[32,64,128]{2,1,0:T(8,128)(2,1)S(1)}, u32[]{:S(2)}, u32[]{:S(2)}) %all-to-all-start.2) | async-done | bytes 524320 | tf_op jit(solution)/shard_map/all_to_all | solution.py:46
  121.0 3.5 %collective-permute-start.14 = (bf16[128,2048]{1,0:T(8,128)(2,1)S(1)}, bf16[128,2048]{1,0:T(8,128)(2,1)S(1)}, u32[]{:S(2)}, u32[]{:S(2)}) collective-permute-start(bf16[128,2048]{1,0:T(8,128)(2,1)S(1)} %reshape.43.refs_0_), channel_id=1, source_target_pairs={{0,7},{1,0},{2,1},{3,2},{4,3},{5,4},{6,5},{7,6},{8,15},{9,8},{10,9... | collective-permute-start | bytes 1572872 | tf_op jit(solution)/shard_map/ppermute | solution.py:24
  124.5 2.2 %copy-done.10 = bf16[1024,2048]{1,0:T(8,128)(2,1)S(1)} copy-done((bf16[1024,2048]{1,0:T(8,128)(2,1)S(1)}, bf16[1024,2048]{1,0:T(8,128)(2,1)}, u32[]{:S(2)}) %copy-start.10) | copy-done | bytes 4194328
  126.7 2.2 %copy-done.13 = bf16[2048,1024]{1,0:T(8,128)(2,1)S(1)} copy-done((bf16[2048,1024]{1,0:T(8,128)(2,1)S(1)}, bf16[2048,1024]{1,0:T(8,128)(2,1)}, u32[]{:S(2)}) %copy-start.13) | copy-done | bytes 4194328
  128.9 1.9 %shard_map.100 = (bf16[64,2048]{1,0:T(8,128)(2,1)S(1)}, bf16[64,2048]{1,0:T(8,128)(2,1)S(1)}) custom-call(s32[3]{0:T(128)S(1)} %pad_add_fusion.flip_ref, bf16[128,2048]{1,0:T(8,128)(2,1)S(1)} %reshape.43.refs_0_, bf16[128,1024]{1,0:T(8,128)(2,1)S(1)} %get-tuple-element.45.refs_1_, bf16[1024,2048]{1,0:T(8,128)(2,1)S(1)} %copy-done.10, ...), custom_call_target="tpu_custom_call" | custom-call | flops 8589934592 | bytes 1048576 | tf_op jit(solution)/shard_map/pallas_call | solution.py:211
  130.7 1.1 collective-permute-start.12
  131.9 3.7 %collective-permute-done.13.refs_0_ = bf16[128,2048]{1,0:T(8,128)(2,1)S(1)} collective-permute-done((bf16[128,2048]{1,0:T(8,128)(2,1)S(1)}, bf16[128,2048]{1,0:T(8,128)(2,1)S(1)}, u32[]{:S(2)}, u32[]{:S(2)}) %collective-permute-start.13) | collective-permute-done | bytes 524320 | tf_op jit(solution)/shard_map/ppermute | solution.py:24
  135.6 2.5 %collective-permute-start.16 = (bf16[64,2048]{1,0:T(8,128)(2,1)S(1)}, bf16[64,2048]{1,0:T(8,128)(2,1)S(1)}, u32[]{:S(2)}, u32[]{:S(2)}) collective-permute-start(bf16[64,2048]{1,0:T(8,128)(2,1)S(1)} %slice_select_fusion.1), channel_id=1, source_target_pairs={{0,1},{1,2},{2,3},{3,4},{4,5},{5,6},{6,7},{7,0},{8,9},{9,10},{10,1... | collective-permute-start | bytes 786440 | tf_op jit(solution)/shard_map/ppermute | solution.py:24
  138.1 1.5 collective-permute-start.17
  139.7 2.9 %shard_map.101 = (bf16[64,2048]{1,0:T(8,128)(2,1)S(1)}, bf16[64,2048]{1,0:T(8,128)(2,1)S(1)}, bf16[64,2048]{1,0:T(8,128)(2,1)S(1)}, bf16[64,2048]{1,0:T(8,128)(2,1)S(1)}) custom-call(s32[3]{0:T(128)S(1)} %pad_add_fusion.flip_ref, bf16[128,2048]{1,0:T(8,128)(2,1)S(1)} %collective-permute-done.13.refs_0_, ...), custom_call_target="tpu_custom_call" | custom-call | flops 17179869184 | bytes 1048576 | tf_op jit(solution)/shard_map/pallas_call | solution.py:211
  142.6 1.1 collective-permute-start.15
  143.8 2.2 %collective-permute-start.20 = (bf16[64,2048]{1,0:T(8,128)(2,1)S(1)}, bf16[64,2048]{1,0:T(8,128)(2,1)S(1)}, u32[]{:S(2)}, u32[]{:S(2)}) collective-permute-start(bf16[64,2048]{1,0:T(8,128)(2,1)S(1)} %get-tuple-element.55), channel_id=1, source_target_pairs={{0,7},{1,0},{2,1},{3,2},{4,3},{5,4},{6,5},{7,6},{8,15},{9,8},{10,9... | collective-permute-start | bytes 786440 | tf_op jit(solution)/shard_map/ppermute | solution.py:24
  146.0 1.8 shard_map.102
  147.8 4.4 %collective-permute-done.15 = bf16[64,2048]{1,0:T(8,128)(2,1)S(1)} collective-permute-done((bf16[64,2048]{1,0:T(8,128)(2,1)S(1)}, bf16[64,2048]{1,0:T(8,128)(2,1)S(1)}, u32[]{:S(2)}, u32[]{:S(2)}) %collective-permute-start.15) | collective-permute-done | bytes 262176 | tf_op jit(solution)/shard_map/ppermute | solution.py:24
  153.0 2.7 %collective-permute-start.21 = (bf16[64,2048]{1,0:T(8,128)(2,1)S(1)}, bf16[64,2048]{1,0:T(8,128)(2,1)S(1)}, u32[]{:S(2)}, u32[]{:S(2)}) collective-permute-start(bf16[64,2048]{1,0:T(8,128)(2,1)S(1)} %add_convert_fusion.2), channel_id=1, source_target_pairs={{0,7},{1,0},{2,1},{3,2},{4,3},{5,4},{6,5},{7,6},{8,15},{9,8},{10,9... | collective-permute-start | bytes 786440 | tf_op jit(solution)/shard_map/ppermute | solution.py:24
  155.7 6.8 %collective-permute-done.18 = bf16[64,2048]{1,0:T(8,128)(2,1)S(1)} collective-permute-done((bf16[64,2048]{1,0:T(8,128)(2,1)S(1)}, bf16[64,2048]{1,0:T(8,128)(2,1)S(1)}, u32[]{:S(2)}, u32[]{:S(2)}) %collective-permute-start.18) | collective-permute-done | bytes 262176 | tf_op jit(solution)/shard_map/ppermute | solution.py:24
  162.7 3.3 %collective-permute-start.22 = (bf16[64,2048]{1,0:T(8,128)(2,1)S(1)}, bf16[64,2048]{1,0:T(8,128)(2,1)S(1)}, u32[]{:S(2)}, u32[]{:S(2)}) collective-permute-start(bf16[64,2048]{1,0:T(8,128)(2,1)S(1)} %add_convert_fusion.1), channel_id=1, source_target_pairs={{0,7},{1,0},{2,1},{3,2},{4,3},{5,4},{6,5},{7,6},{8,15},{9,8},{10,9... | collective-permute-start | bytes 786440 | tf_op jit(solution)/shard_map/ppermute | solution.py:24
  166.0 4.2 %collective-permute-done.19 = bf16[64,2048]{1,0:T(8,128)(2,1)S(1)} collective-permute-done((bf16[64,2048]{1,0:T(8,128)(2,1)S(1)}, bf16[64,2048]{1,0:T(8,128)(2,1)S(1)}, u32[]{:S(2)}, u32[]{:S(2)}) %collective-permute-start.19) | collective-permute-done | bytes 262176 | tf_op jit(solution)/shard_map/ppermute | solution.py:24
  170.5 14.0 %all_to_all.21 = bf16[16,64,128]{2,1,0:T(8,128)(2,1)S(1)} all-to-all(bf16[16,64,128]{2,1,0:T(8,128)(2,1)S(1)} %reshape.44), channel_id=1, replica_groups={{0,8,16,24,32,40,48,56,64,72,80,88,96,104,112,120},{1,9,17,25,33,41,49,..., dimensions={0} | all-to-all | bytes 524288 | tf_op jit(solution)/shard_map/all_to_all | solution.py:33
  184.6 1.6 shard_map.103
  (72 shorter events, 12.3 us)
Async XLA Ops:
  1.3 1.0 copy-start
  2.3 0.7 copy-start.7
  4.6 29.6 %all-to-all-start = ((bf16[32,64,128]{2,1,0:T(8,128)(2,1)}), bf16[32,64,128]{2,1,0:T(8,128)(2,1)S(1)}, u32[]{:S(2)}, u32[]{:S(2)}) async-start(bf16[32,64,128]{2,1,0:T(8,128)(2,1)} %reshape.38), calls=%async_computation | async-start | bytes 1048576 | tf_op jit(solution)/shard_map/all_to_all | solution.py:46
  34.4 17.9 %collective-permute-start.1 = (bf16[128,2048]{1,0:T(8,128)(2,1)S(1)}, bf16[128,2048]{1,0:T(8,128)(2,1)S(1)}, u32[]{:S(2)}, u32[]{:S(2)}) collective-permute-start(bf16[128,2048]{1,0:T(8,128)(2,1)S(1)} %reshape.39.refs_0_), channel_id=1, source_target_pairs={{0,1},{1,2},{2,3},{3,4},{4,5},{5,6},{6,7},{7,0},{8,9},{9,10},{10,1... | collective-permute-start | bytes 1572872 | tf_op jit(solution)/shard_map/ppermute | solution.py:24
  39.9 15.0 %collective-permute-start.2 = (bf16[128,2048]{1,0:T(8,128)(2,1)S(1)}, bf16[128,2048]{1,0:T(8,128)(2,1)S(1)}, u32[]{:S(2)}, u32[]{:S(2)}) collective-permute-start(bf16[128,2048]{1,0:T(8,128)(2,1)S(1)} %reshape.39.refs_0_), channel_id=1, source_target_pairs={{0,7},{1,0},{2,1},{3,2},{4,3},{5,4},{6,5},{7,6},{8,15},{9,8},{10,9... | collective-permute-start | bytes 1572872 | tf_op jit(solution)/shard_map/ppermute | solution.py:24
  39.9 2.2 %copy-start.2 = (bf16[1,2048,1024]{2,1,0:T(8,128)(2,1)S(1)}, bf16[1,2048,1024]{2,1,0:T(8,128)(2,1)}, u32[]{:S(2)}) copy-start(bf16[1,2048,1024]{2,1,0:T(8,128)(2,1)} %param.11) | copy-start | bytes 12582916
  42.1 2.2 %copy-start.5 = (bf16[1,1024,2048]{2,1,0:T(8,128)(2,1)S(1)}, bf16[1,1024,2048]{2,1,0:T(8,128)(2,1)}, u32[]{:S(2)}) copy-start(bf16[1,1024,2048]{2,1,0:T(8,128)(2,1)} %param.12) | copy-start | bytes 12582916
  44.3 11.5 %copy-start.3 = (bf16[1,2048,1024]{2,1,0:T(8,128)(2,1)S(1)}, bf16[1,2048,1024]{2,1,0:T(8,128)(2,1)}, u32[]{:S(2)}) copy-start(bf16[1,2048,1024]{2,1,0:T(8,128)(2,1)} %param.11) | copy-start | bytes 12582916
  46.2 12.5 %collective-permute-start = (bf16[64,2048]{1,0:T(8,128)(2,1)S(1)}, bf16[64,2048]{1,0:T(8,128)(2,1)S(1)}, u32[]{:S(2)}, u32[]{:S(2)}) collective-permute-start(bf16[64,2048]{1,0:T(8,128)(2,1)S(1)} %get-tuple-element.35), channel_id=1, source_target_pairs={{0,1},{1,2},{2,3},{3,4},{4,5},{5,6},{6,7},{7,0},{8,9},{9,10},{10,1... | collective-permute-start | bytes 786440 | tf_op jit(solution)/shard_map/ppermute | solution.py:24
  52.3 11.2 %collective-permute-start.4 = (bf16[64,2048]{1,0:T(8,128)(2,1)S(1)}, bf16[64,2048]{1,0:T(8,128)(2,1)S(1)}, u32[]{:S(2)}, u32[]{:S(2)}) collective-permute-start(bf16[64,2048]{1,0:T(8,128)(2,1)S(1)} %slice_select_fusion.3), channel_id=1, source_target_pairs={{0,1},{1,2},{2,3},{3,4},{4,5},{5,6},{6,7},{7,0},{8,9},{9,10},{10,1... | collective-permute-start | bytes 786440 | tf_op jit(solution)/shard_map/ppermute | solution.py:24
  54.9 9.1 %collective-permute-start.5 = (bf16[64,2048]{1,0:T(8,128)(2,1)S(1)}, bf16[64,2048]{1,0:T(8,128)(2,1)S(1)}, u32[]{:S(2)}, u32[]{:S(2)}) collective-permute-start(bf16[64,2048]{1,0:T(8,128)(2,1)S(1)} %slice_select_fusion.2), channel_id=1, source_target_pairs={{0,7},{1,0},{2,1},{3,2},{4,3},{5,4},{6,5},{7,6},{8,15},{9,8},{10,9... | collective-permute-start | bytes 786440 | tf_op jit(solution)/shard_map/ppermute | solution.py:24
  58.7 8.1 %collective-permute-start.3 = (bf16[64,2048]{1,0:T(8,128)(2,1)S(1)}, bf16[64,2048]{1,0:T(8,128)(2,1)S(1)}, u32[]{:S(2)}, u32[]{:S(2)}) collective-permute-start(bf16[64,2048]{1,0:T(8,128)(2,1)S(1)} %add_convert_fusion.11), channel_id=1, source_target_pairs={{0,1},{1,2},{2,3},{3,4},{4,5},{5,6},{6,7},{7,0},{8,9},{9,10},{10,1... | collective-permute-start | bytes 786440 | tf_op jit(solution)/shard_map/ppermute | solution.py:24
  60.5 17.8 %copy-start.14 = (bf16[2,128,1024]{2,1,0:T(8,128)(2,1)S(1)}, bf16[2,128,1024]{2,1,0:T(8,128)(2,1)}, u32[]{:S(2)}) copy-start(bf16[2,128,1024]{2,1,0:T(8,128)(2,1)} %param.13) | copy-start | bytes 1572868
  60.5 9.1 %collective-permute-start.8 = (bf16[64,2048]{1,0:T(8,128)(2,1)S(1)}, bf16[64,2048]{1,0:T(8,128)(2,1)S(1)}, u32[]{:S(2)}, u32[]{:S(2)}) collective-permute-start(bf16[64,2048]{1,0:T(8,128)(2,1)S(1)} %get-tuple-element.39), channel_id=1, source_target_pairs={{0,7},{1,0},{2,1},{3,2},{4,3},{5,4},{6,5},{7,6},{8,15},{9,8},{10,9... | collective-permute-start | bytes 786440 | tf_op jit(solution)/shard_map/ppermute | solution.py:24
  65.9 31.3 %copy-start.1 = (bf16[1,128,2048]{2,1,0:T(8,128)(2,1)S(1)}, bf16[1,128,2048]{2,1,0:T(8,128)(2,1)}, u32[]{:S(2)}) copy-start(bf16[1,128,2048]{2,1,0:T(8,128)(2,1)} %param.7) | copy-start | bytes 1572868
  65.9 31.3 %copy-start.8 = (f32[1,128,2]{1,2,0:T(2,128)S(1)}, f32[1,128,2]{1,2,0:T(2,128)}, u32[]{:S(2)}) copy-start(f32[1,128,2]{1,2,0:T(2,128)} %param.9) | copy-start | bytes 3076
  66.9 7.8 %collective-permute-start.6 = (bf16[64,2048]{1,0:T(8,128)(2,1)S(1)}, bf16[64,2048]{1,0:T(8,128)(2,1)S(1)}, u32[]{:S(2)}, u32[]{:S(2)}) collective-permute-start(bf16[64,2048]{1,0:T(8,128)(2,1)S(1)} %add_convert_fusion.10), channel_id=1, source_target_pairs={{0,1},{1,2},{2,3},{3,4},{4,5},{5,6},{6,7},{7,0},{8,9},{9,10},{10,1... | collective-permute-start | bytes 786440 | tf_op jit(solution)/shard_map/ppermute | solution.py:24
  69.8 7.0 %collective-permute-start.9 = (bf16[64,2048]{1,0:T(8,128)(2,1)S(1)}, bf16[64,2048]{1,0:T(8,128)(2,1)S(1)}, u32[]{:S(2)}, u32[]{:S(2)}) collective-permute-start(bf16[64,2048]{1,0:T(8,128)(2,1)S(1)} %add_convert_fusion.8), channel_id=1, source_target_pairs={{0,7},{1,0},{2,1},{3,2},{4,3},{5,4},{6,5},{7,6},{8,15},{9,8},{10,9... | collective-permute-start | bytes 786440 | tf_op jit(solution)/shard_map/ppermute | solution.py:24
  74.9 7.8 %collective-permute-start.7 = (bf16[64,2048]{1,0:T(8,128)(2,1)S(1)}, bf16[64,2048]{1,0:T(8,128)(2,1)}, u32[]{:S(2)}, u32[]{:S(2)}) collective-permute-start(bf16[64,2048]{1,0:T(8,128)(2,1)S(1)} %add_convert_fusion.9), channel_id=1, source_target_pairs={{0,1},{1,2},{2,3},{3,4},{4,5},{5,6},{6,7},{7,0},{8,9},{9,10},{10,1... | collective-permute-start | bytes 786440 | tf_op jit(solution)/shard_map/ppermute | solution.py:24
  76.8 6.5 %collective-permute-start.10 = (bf16[64,2048]{1,0:T(8,128)(2,1)S(1)}, bf16[64,2048]{1,0:T(8,128)(2,1)S(1)}, u32[]{:S(2)}, u32[]{:S(2)}) collective-permute-start(bf16[64,2048]{1,0:T(8,128)(2,1)S(1)} %add_convert_fusion.7), channel_id=1, source_target_pairs={{0,7},{1,0},{2,1},{3,2},{4,3},{5,4},{6,5},{7,6},{8,15},{9,8},{10,9... | collective-permute-start | bytes 786440 | tf_op jit(solution)/shard_map/ppermute | solution.py:24
  79.1 18.1 %collective-permute-start.11 = (bf16[128,1024]{1,0:T(8,128)(2,1)}, bf16[128,1024]{1,0:T(8,128)(2,1)S(1)}, u32[]{:S(2)}, u32[]{:S(2)}) collective-permute-start(bf16[128,1024]{1,0:T(8,128)(2,1)} %get-tuple-element.59), channel_id=1, source_target_pairs={{0,128},{128,0},{1,129},{129,1},{2,130},{130,2},{3,131},{131,3},{4... | collective-permute-start | bytes 786440 | tf_op jit(solution)/shard_map/ppermute | solution.py:233
  83.2 0.7 copy-start.15
  100.8 19.9 %all-to-all-start.2 = ((bf16[32,64,128]{2,1,0:T(8,128)(2,1)}), bf16[32,64,128]{2,1,0:T(8,128)(2,1)S(1)}, u32[]{:S(2)}, u32[]{:S(2)}) async-start(bf16[32,64,128]{2,1,0:T(8,128)(2,1)} %reshape.42), calls=%async_computation.2 | async-start | bytes 1048576 | tf_op jit(solution)/shard_map/all_to_all | solution.py:46
  106.8 2.2 %copy-start.4 = (bf16[1,2048,1024]{2,1,0:T(8,128)(2,1)S(1)}, bf16[1,2048,1024]{2,1,0:T(8,128)(2,1)}, u32[]{:S(2)}) copy-start(bf16[1,2048,1024]{2,1,0:T(8,128)(2,1)} %param.11) | copy-start | bytes 12582916
  109.0 2.2 %copy-start.6 = (bf16[1,1024,2048]{2,1,0:T(8,128)(2,1)S(1)}, bf16[1,1024,2048]{2,1,0:T(8,128)(2,1)}, u32[]{:S(2)}) copy-start(bf16[1,1024,2048]{2,1,0:T(8,128)(2,1)} %param.12) | copy-start | bytes 12582916
  113.6 2.0 %copy-start.9 = (bf16[1024,2048]{1,0:T(8,128)(2,1)}, bf16[1024,2048]{1,0:T(8,128)(2,1)S(1)}, u32[]{:S(2)}) copy-start(bf16[1024,2048]{1,0:T(8,128)(2,1)S(1)} %get-tuple-element.46.refs_2_.refs_3_) | copy-start | bytes 12582916
  115.6 2.0 %copy-start.12 = (bf16[2048,1024]{1,0:T(8,128)(2,1)}, bf16[2048,1024]{1,0:T(8,128)(2,1)S(1)}, u32[]{:S(2)}) copy-start(bf16[2048,1024]{1,0:T(8,128)(2,1)S(1)} %get-tuple-element.47.refs_3_.refs_4_) | copy-start | bytes 12582916
  120.9 14.7 %collective-permute-start.13 = (bf16[128,2048]{1,0:T(8,128)(2,1)S(1)}, bf16[128,2048]{1,0:T(8,128)(2,1)S(1)}, u32[]{:S(2)}, u32[]{:S(2)}) collective-permute-start(bf16[128,2048]{1,0:T(8,128)(2,1)S(1)} %reshape.43.refs_0_), channel_id=1, source_target_pairs={{0,1},{1,2},{2,3},{3,4},{4,5},{5,6},{6,7},{7,0},{8,9},{9,10},{10,1... | collective-permute-start | bytes 1572872 | tf_op jit(solution)/shard_map/ppermute | solution.py:24
  121.0 17.1 %collective-permute-start.14 = (bf16[128,2048]{1,0:T(8,128)(2,1)S(1)}, bf16[128,2048]{1,0:T(8,128)(2,1)S(1)}, u32[]{:S(2)}, u32[]{:S(2)}) collective-permute-start(bf16[128,2048]{1,0:T(8,128)(2,1)S(1)} %reshape.43.refs_0_), channel_id=1, source_target_pairs={{0,7},{1,0},{2,1},{3,2},{4,3},{5,4},{6,5},{7,6},{8,15},{9,8},{10,9... | collective-permute-start | bytes 1572872 | tf_op jit(solution)/shard_map/ppermute | solution.py:24
  124.5 2.2 %copy-start.10 = (bf16[1024,2048]{1,0:T(8,128)(2,1)S(1)}, bf16[1024,2048]{1,0:T(8,128)(2,1)}, u32[]{:S(2)}) copy-start(bf16[1024,2048]{1,0:T(8,128)(2,1)} %copy-done.9) | copy-start | bytes 12582916
  126.7 2.2 %copy-start.13 = (bf16[2048,1024]{1,0:T(8,128)(2,1)S(1)}, bf16[2048,1024]{1,0:T(8,128)(2,1)}, u32[]{:S(2)}) copy-start(bf16[2048,1024]{1,0:T(8,128)(2,1)} %copy-done.12) | copy-start | bytes 12582916
  128.9 10.8 %copy-start.11 = (bf16[1024,2048]{1,0:T(8,128)(2,1)S(1)}, bf16[1024,2048]{1,0:T(8,128)(2,1)}, u32[]{:S(2)}) copy-start(bf16[1024,2048]{1,0:T(8,128)(2,1)} %copy-done.9) | copy-start | bytes 12582916
  130.7 11.8 %collective-permute-start.12 = (bf16[64,2048]{1,0:T(8,128)(2,1)S(1)}, bf16[64,2048]{1,0:T(8,128)(2,1)S(1)}, u32[]{:S(2)}, u32[]{:S(2)}) collective-permute-start(bf16[64,2048]{1,0:T(8,128)(2,1)S(1)} %get-tuple-element.49), channel_id=1, source_target_pairs={{0,1},{1,2},{2,3},{3,4},{4,5},{5,6},{6,7},{7,0},{8,9},{9,10},{10,1... | collective-permute-start | bytes 786440 | tf_op jit(solution)/shard_map/ppermute | solution.py:24
  135.6 10.3 %collective-permute-start.16 = (bf16[64,2048]{1,0:T(8,128)(2,1)S(1)}, bf16[64,2048]{1,0:T(8,128)(2,1)S(1)}, u32[]{:S(2)}, u32[]{:S(2)}) collective-permute-start(bf16[64,2048]{1,0:T(8,128)(2,1)S(1)} %slice_select_fusion.1), channel_id=1, source_target_pairs={{0,1},{1,2},{2,3},{3,4},{4,5},{5,6},{6,7},{7,0},{8,9},{9,10},{10,1... | collective-permute-start | bytes 786440 | tf_op jit(solution)/shard_map/ppermute | solution.py:24
  138.1 7.8 %collective-permute-start.17 = (bf16[64,2048]{1,0:T(8,128)(2,1)S(1)}, bf16[64,2048]{1,0:T(8,128)(2,1)S(1)}, u32[]{:S(2)}, u32[]{:S(2)}) collective-permute-start(bf16[64,2048]{1,0:T(8,128)(2,1)S(1)} %slice_select_fusion), channel_id=1, source_target_pairs={{0,7},{1,0},{2,1},{3,2},{4,3},{5,4},{6,5},{7,6},{8,15},{9,8},{10,9... | collective-permute-start | bytes 786440 | tf_op jit(solution)/shard_map/ppermute | solution.py:24
  142.6 9.5 %collective-permute-start.15 = (bf16[64,2048]{1,0:T(8,128)(2,1)S(1)}, bf16[64,2048]{1,0:T(8,128)(2,1)S(1)}, u32[]{:S(2)}, u32[]{:S(2)}) collective-permute-start(bf16[64,2048]{1,0:T(8,128)(2,1)S(1)} %add_convert_fusion.5), channel_id=1, source_target_pairs={{0,1},{1,2},{2,3},{3,4},{4,5},{5,6},{6,7},{7,0},{8,9},{9,10},{10,1... | collective-permute-start | bytes 786440 | tf_op jit(solution)/shard_map/ppermute | solution.py:24
  143.8 9.2 %collective-permute-start.20 = (bf16[64,2048]{1,0:T(8,128)(2,1)S(1)}, bf16[64,2048]{1,0:T(8,128)(2,1)S(1)}, u32[]{:S(2)}, u32[]{:S(2)}) collective-permute-start(bf16[64,2048]{1,0:T(8,128)(2,1)S(1)} %get-tuple-element.55), channel_id=1, source_target_pairs={{0,7},{1,0},{2,1},{3,2},{4,3},{5,4},{6,5},{7,6},{8,15},{9,8},{10,9... | collective-permute-start | bytes 786440 | tf_op jit(solution)/shard_map/ppermute | solution.py:24
  152.2 10.2 %collective-permute-start.18 = (bf16[64,2048]{1,0:T(8,128)(2,1)S(1)}, bf16[64,2048]{1,0:T(8,128)(2,1)S(1)}, u32[]{:S(2)}, u32[]{:S(2)}) collective-permute-start(bf16[64,2048]{1,0:T(8,128)(2,1)S(1)} %add_convert_fusion.4), channel_id=1, source_target_pairs={{0,1},{1,2},{2,3},{3,4},{4,5},{5,6},{6,7},{7,0},{8,9},{9,10},{10,1... | collective-permute-start | bytes 786440 | tf_op jit(solution)/shard_map/ppermute | solution.py:24
  153.0 9.7 %collective-permute-start.21 = (bf16[64,2048]{1,0:T(8,128)(2,1)S(1)}, bf16[64,2048]{1,0:T(8,128)(2,1)S(1)}, u32[]{:S(2)}, u32[]{:S(2)}) collective-permute-start(bf16[64,2048]{1,0:T(8,128)(2,1)S(1)} %add_convert_fusion.2), channel_id=1, source_target_pairs={{0,7},{1,0},{2,1},{3,2},{4,3},{5,4},{6,5},{7,6},{8,15},{9,8},{10,9... | collective-permute-start | bytes 786440 | tf_op jit(solution)/shard_map/ppermute | solution.py:24
  162.6 7.7 %collective-permute-start.19 = (bf16[64,2048]{1,0:T(8,128)(2,1)S(1)}, bf16[64,2048]{1,0:T(8,128)(2,1)S(1)}, u32[]{:S(2)}, u32[]{:S(2)}) collective-permute-start(bf16[64,2048]{1,0:T(8,128)(2,1)S(1)} %add_convert_fusion.3), channel_id=1, source_target_pairs={{0,1},{1,2},{2,3},{3,4},{4,5},{5,6},{6,7},{7,0},{8,9},{9,10},{10,1... | collective-permute-start | bytes 786440 | tf_op jit(solution)/shard_map/ppermute | solution.py:24
  162.7 7.5 %collective-permute-start.22 = (bf16[64,2048]{1,0:T(8,128)(2,1)S(1)}, bf16[64,2048]{1,0:T(8,128)(2,1)S(1)}, u32[]{:S(2)}, u32[]{:S(2)}) collective-permute-start(bf16[64,2048]{1,0:T(8,128)(2,1)S(1)} %add_convert_fusion.1), channel_id=1, source_target_pairs={{0,7},{1,0},{2,1},{3,2},{4,3},{5,4},{6,5},{7,6},{8,15},{9,8},{10,9... | collective-permute-start | bytes 786440 | tf_op jit(solution)/shard_map/ppermute | solution.py:24
where the time goes:
time: 187 us; the launch traced here: 186 us
  starting transfers between devices  60.2 us (32%)
  waiting for transfers between devices  52.7 us (28%)
  blocking collectives  25.9 us (14%)
  local copies, waits for them, and re-layouts  22.5 us (12%)
  Pallas kernels  20.3 us (11%)
  other arithmetic  2.82 us (2%)
    ppermute x22, starting transfers between devices, hop(): return lax.ppermute(value, 'expert', pairs)  40.1 us
    ppermute x22, waiting for transfers between devices, hop(): return lax.ppermute(value, 'expert', pairs)  34.4 us
    all_to_all x2, blocking collectives, swap_plane(): lax.all_to_all(packed, 'expert', split_axis=0, concat_axis=0, axis_index_...  25.9 us
    pallas_call x10, Pallas kernels, call(): pl.pallas_call(kernel, out_shape=outs, in_specs=[pl.BlockSpec(memory_spac...  20.3 us
    all_to_all x2, starting transfers between devices, swap_pair(): lax.all_to_all(packed, 'expert', split_axis=0, concat_axis=0, axis_index_...  20.2 us
    unnamed x32, local copies, waits for them, and re-layouts  19.5 us
    all_to_all x2, waiting for transfers between devices, swap_pair(): lax.all_to_all(packed, 'expert', split_axis=0, concat_axis=0, axis_index_...  18.3 us
  transfers between devices with their start and end apart: 25, of which 13 were waited for; matrix products, arithmetic and copies ran while one was open for 2% of the time, Pallas kernels for 8%

commit v1 on v0

--- a/solution.py
+++ b/solution.py
@@ -12,7 +12,7 @@
 LIVE = 16
 SLOTS = LIVE * CAP
 EPS = 1e-05
-COST = 32
+COST = 4
 BF = jnp.bfloat16
 F32 = jnp.float32
 VMEM_LIMIT = 16 * 2**20
@@ -167,6 +167,10 @@
     out_ref[...] = (upstream_ref[...].astype(F32) + norm_back(normed, scale, d_normed)).astype(BF)
 
 
+def turned_dot(a, b):
+    return lax.dot_general(a, b, (((1,), (1,)), ((), ())), preferred_element_type=F32)
+
+
 def stack(refs):
     return jnp.concatenate([ref[...] for ref in refs], axis=0) if len(refs) > 1 else refs[0][...]
 
@@ -194,16 +198,11 @@
 
 
 def backward_kernel(count, start, flip_ref, *refs):
-    blocks, (act_ref, w_in_t_ref, w_out_t_ref) = refs[:count], refs[count : count + 3]
-    d_act = jnp.dot(stack(blocks), w_out_t_ref[...], preferred_element_type=F32)
+    blocks, (act_ref, w_in_ref, w_out_ref) = refs[:count], refs[count : count + 3]
+    d_act = turned_dot(stack(blocks), w_out_ref[...])
     d_pre = jnp.where(act_ref[...] > 0, d_act, 0.0).astype(BF)
-    terms = jnp.dot(d_pre, w_in_t_ref[...], preferred_element_type=F32)
+    terms = turned_dot(d_pre, w_in_ref[...])
     spread(refs[count + 3 :], terms, flip_ref, start)
-
-
-def turn_kernel(w_in_ref, w_out_ref, w_in_t_ref, w_out_t_ref):
-    w_in_t_ref[...] = w_in_ref[...].T
-    w_out_t_ref[...] = w_out_ref[...].T
 
 
 def call(kernel, outs, scalars, *arrays, flops=0, limit=VMEM_LIMIT):
@@ -236,8 +235,6 @@
         dispatch_kernel, [twice, table, table], 2, lengths, section_id, routes[0].T, source
     )
 
-    turned = [jax.ShapeDtypeStruct(w.shape[::-1], BF) for w in (w_in, w_out)]
-    w_in_t, w_out_t = call(turn_kernel, turned, 0, w_in, w_out, limit=32 * 2**20)
     hidden_units = w_in.shape[1]
     plane = lax.axis_index("expert") % SPLIT
     flips = jnp.stack([(plane + d) % SPLIT // (SPLIT // 2) for d in (0, -1, 1)]).astype(jnp.int32)
@@ -267,7 +264,7 @@
         return terms
 
     def backward(key, blocks):
-        return run(backward_kernel, key, blocks, [acts[key], w_in_t, w_out_t], [])[1]
+        return run(backward_kernel, key, blocks, [acts[key], w_in, w_out], [])[1]
 
     y = swap_plane(exchange(rows, flips, forward))
 

time: 187 us -> 182 us (0.973)
  blocking collectives: 25.9 us -> 76.6 us
  waiting for transfers between devices: 52.7 us -> 29.4 us
  starting transfers between devices: 60.2 us -> 38.3 us
  local copies, waits for them, and re-layouts: 22.5 us -> 11.9 us
    all_to_all x0 -> x2, blocking collectives: none -> 52.7 us  [swap_pair(): lax.all_to_all(packed, 'expert', split_axis=0, concat_axis=0, axis_index_...]
    all_to_all x2 -> x0, starting transfers between devices: 20.2 us -> none  [swap_pair(): lax.all_to_all(packed, 'expert', split_axis=0, concat_axis=0, axis_index_...]
    all_to_all x2 -> x0, waiting for transfers between devices: 18.3 us -> none  [swap_pair(): lax.all_to_all(packed, 'expert', split_axis=0, concat_axis=0, axis_index_...]
    unnamed x32 -> x20, local copies, waits for them, and re-layouts: 19.5 us -> 10.5 us
    ppermute x22, waiting for transfers between devices: 34.4 us -> 29.4 us  [hop(): return lax.ppermute(value, 'expert', pairs)]
    all_to_all x2, blocking collectives: 25.9 us -> 23.9 us  [swap_plane(): lax.all_to_all(packed, 'expert', split_axis=0, concat_axis=0, axis_index_...]
    pallas_call x10 -> x9, Pallas kernels: 20.3 us -> 21.2 us  [call(): pl.pallas_call(kernel, out_shape=outs, in_specs=[pl.BlockSpec(memory_spac...]
  transfers between devices with their start and end apart: 25 -> 23, of which waited for: 13 -> 11; matrix products, arithmetic and copies ran while one was open for 2% -> 2% of each run, Pallas kernels for 8% -> 9%
where the time goes in v1:
time: 182 us
  blocking collectives  76.6 us (42%)
  starting transfers between devices  38.3 us (21%)
  waiting for transfers between devices  29.4 us (16%)
  Pallas kernels  21.2 us (12%)
  local copies, waits for them, and re-layouts  11.9 us (7%)
  other arithmetic  2.82 us (2%)
    all_to_all x2, blocking collectives, swap_pair(): lax.all_to_all(packed, 'expert', split_axis=0, concat_axis=0, axis_index_...  52.7 us
    ppermute x22, starting transfers between devices, hop(): return lax.ppermute(value, 'expert', pairs)  38.3 us
    ppermute x22, waiting for transfers between devices, hop(): return lax.ppermute(value, 'expert', pairs)  29.4 us
    all_to_all x2, blocking collectives, swap_plane(): lax.all_to_all(packed, 'expert', split_axis=0, concat_axis=0, axis_index_...  23.9 us
    pallas_call x9, Pallas kernels, call(): pl.pallas_call(kernel, out_shape=outs, in_specs=[pl.BlockSpec(memory_spac...  21.2 us
    unnamed x20, local copies, waits for them, and re-layouts  10.5 us
  transfers between devices with their start and end apart: 23, of which 11 were waited for; matrix products, arithmetic and copies ran while one was open for 2% of the time, Pallas kernels for 9%

profile of v1, /device:TPU:8, one launch (start us, length us, event | category | flops | bytes accessed | tf_op | source)
XLA Modules:
  0.0 181.7 jit_solution(2198735367815911528)
XLA Ops:
  1.3 1.0 copy-done.5
  2.3 0.7 copy-done.7
  3.0 0.6 shard_map.94
  3.6 0.2 reshape.38
  3.8 29.4 %all_to_all.20 = bf16[32,64,128]{2,1,0:T(8,128)(2,1)S(1)} all-to-all(bf16[32,64,128]{2,1,0:T(8,128)(2,1)S(1)} %reshape.38), channel_id=1, replica_groups={{0,8,16,24,32,40,48,56,64,72,80,88,96,104,112,120,4,12,20,28,36,44,52,6..., dimensions={0} | all-to-all | bytes 1048576 | tf_op jit(solution)/shard_map/all_to_all | solution.py:46
  33.4 5.5 %collective-permute-start.1 = (bf16[128,2048]{1,0:T(8,128)(2,1)S(1)}, bf16[128,2048]{1,0:T(8,128)(2,1)S(1)}, u32[]{:S(2)}, u32[]{:S(2)}) collective-permute-start(bf16[128,2048]{1,0:T(8,128)(2,1)S(1)} %reshape.39.refs_0_), channel_id=1, source_target_pairs={{0,1},{1,2},{2,3},{3,4},{4,5},{5,6},{6,7},{7,0},{8,9},{9,10},{10,1... | collective-permute-start | bytes 1572872 | tf_op jit(solution)/shard_map/ppermute | solution.py:24
  39.0 2.2 %copy-done = bf16[1,2048,1024]{2,1,0:T(8,128)(2,1)S(1)} copy-done((bf16[1,2048,1024]{2,1,0:T(8,128)(2,1)S(1)}, bf16[1,2048,1024]{2,1,0:T(8,128)(2,1)}, u32[]{:S(2)}) %copy-start) | copy-done | bytes 4194328
  41.2 2.2 %copy-done.3 = bf16[1,1024,2048]{2,1,0:T(8,128)(2,1)S(1)} copy-done((bf16[1,1024,2048]{2,1,0:T(8,128)(2,1)S(1)}, bf16[1,1024,2048]{2,1,0:T(8,128)(2,1)}, u32[]{:S(2)}) %copy-start.3) | copy-done | bytes 4194328
  43.4 1.9 %shard_map.95 = (bf16[128,1024]{1,0:T(8,128)(2,1)S(1)}, bf16[64,2048]{1,0:T(8,128)(2,1)S(1)}, bf16[64,2048]{1,0:T(8,128)(2,1)S(1)}) custom-call(s32[3]{0:T(128)S(1)} %pad_add_fusion.flip_ref, bf16[128,2048]{1,0:T(8,128)(2,1)S(1)} %reshape.39.refs_0_, bf16[2048,1024]{1,0:T(8,128)(2,1)S(1)} %bitcast.22, bf16[1024,2048]{1,0:T(8,128)(2,1)S(1)} %bitcast.28), custom_call_target="tpu_custom_call" | custom-call | flops 1073741824 | bytes 1048576 | tf_op jit(solution)/shard_map/pallas_call | solution.py:210
  45.3 2.1 %collective-permute-start = (bf16[64,2048]{1,0:T(8,128)(2,1)S(1)}, bf16[64,2048]{1,0:T(8,128)(2,1)S(1)}, u32[]{:S(2)}, u32[]{:S(2)}) collective-permute-start(bf16[64,2048]{1,0:T(8,128)(2,1)S(1)} %get-tuple-element.33), channel_id=1, source_target_pairs={{0,1},{1,2},{2,3},{3,4},{4,5},{5,6},{6,7},{7,0},{8,9},{9,10},{10,1... | collective-permute-start | bytes 786440 | tf_op jit(solution)/shard_map/ppermute | solution.py:24
  47.4 3.9 %collective-permute-done.1.refs_0_ = bf16[128,2048]{1,0:T(8,128)(2,1)S(1)} collective-permute-done((bf16[128,2048]{1,0:T(8,128)(2,1)S(1)}, bf16[128,2048]{1,0:T(8,128)(2,1)S(1)}, u32[]{:S(2)}, u32[]{:S(2)}) %collective-permute-start.1) | collective-permute-done | bytes 524320 | tf_op jit(solution)/shard_map/ppermute | solution.py:24
  51.3 2.6 %collective-permute-start.4 = (bf16[64,2048]{1,0:T(8,128)(2,1)S(1)}, bf16[64,2048]{1,0:T(8,128)(2,1)S(1)}, u32[]{:S(2)}, u32[]{:S(2)}) collective-permute-start(bf16[64,2048]{1,0:T(8,128)(2,1)S(1)} %slice_select_fusion.3), channel_id=1, source_target_pairs={{0,1},{1,2},{2,3},{3,4},{4,5},{5,6},{6,7},{7,0},{8,9},{9,10},{10,1... | collective-permute-start | bytes 786440 | tf_op jit(solution)/shard_map/ppermute | solution.py:24
  53.9 0.8 collective-permute-start.5
  54.8 2.9 %shard_map.96 = (bf16[256,1024]{1,0:T(8,128)(2,1)S(1)}, bf16[64,2048]{1,0:T(8,128)(2,1)S(1)}, bf16[64,2048]{1,0:T(8,128)(2,1)S(1)}, bf16[64,2048]{1,0:T(8,128)(2,1)S(1)}, bf16[64,2048]{1,0:T(8,128)(2,1)S(1)}) custom-call(s32[3]{0:T(128)S(1)} %pad_add_fusion.flip_ref, bf16[128,2048]{1,0:T(8,128)(2,1)S(1)} %collective-permute-done.1.refs_0_, ...), custom_call_target="tpu_custom_call" | custom-call | flops 2147483648 | bytes 1048576 | tf_op jit(solution)/shard_map/pallas_call | solution.py:210
  57.8 1.8 collective-permute-start.3
  59.5 1.6 collective-permute-start.8
  61.1 1.4 collective-permute-done.4.refs_0_
  62.5 0.5 collective-permute-done.5.refs_1_
  63.0 1.9 %shard_map.97 = (bf16[128,1024]{1,0:T(8,128)(2,1)S(1)}, bf16[64,2048]{1,0:T(8,128)(2,1)S(1)}, bf16[64,2048]{1,0:T(8,128)(2,1)S(1)}) custom-call(s32[3]{0:T(128)S(1)} %pad_add_fusion.flip_ref, bf16[64,2048]{1,0:T(8,128)(2,1)S(1)} %collective-permute-done.4.refs_0_, bf16[64,2048]{1,0:T(8,128)(2,1)S(1)} %collective-permute-done.5.refs_1_, ...), custom_call_target="tpu_custom_call" | custom-call | flops 1073741824 | bytes 1048576 | tf_op jit(solution)/shard_map/pallas_call | solution.py:210
  65.0 0.9 collective-permute-done.3
  66.0 2.7 %collective-permute-start.6 = (bf16[64,2048]{1,0:T(8,128)(2,1)S(1)}, bf16[64,2048]{1,0:T(8,128)(2,1)S(1)}, u32[]{:S(2)}, u32[]{:S(2)}) collective-permute-start(bf16[64,2048]{1,0:T(8,128)(2,1)S(1)} %add_convert_fusion.10), channel_id=1, source_target_pairs={{0,1},{1,2},{2,3},{3,4},{4,5},{5,6},{6,7},{7,0},{8,9},{9,10},{10,1... | collective-permute-start | bytes 786440 | tf_op jit(solution)/shard_map/ppermute | solution.py:24
  68.8 0.8 collective-permute-start.9
  69.6 4.2 %collective-permute-done.6 = bf16[64,2048]{1,0:T(8,128)(2,1)S(1)} collective-permute-done((bf16[64,2048]{1,0:T(8,128)(2,1)S(1)}, bf16[64,2048]{1,0:T(8,128)(2,1)S(1)}, u32[]{:S(2)}, u32[]{:S(2)}) %collective-permute-start.6) | collective-permute-done | bytes 262176 | tf_op jit(solution)/shard_map/ppermute | solution.py:24
  73.9 1.8 %collective-permute-start.7 = (bf16[64,2048]{1,0:T(8,128)(2,1)S(1)}, bf16[64,2048]{1,0:T(8,128)(2,1)}, u32[]{:S(2)}, u32[]{:S(2)}) collective-permute-start(bf16[64,2048]{1,0:T(8,128)(2,1)S(1)} %add_convert_fusion.9), channel_id=1, source_target_pairs={{0,1},{1,2},{2,3},{3,4},{4,5},{5,6},{6,7},{7,0},{8,9},{9,10},{10,1... | collective-permute-start | bytes 786440 | tf_op jit(solution)/shard_map/ppermute | solution.py:24
  75.8 1.5 collective-permute-start.10
  77.3 0.7 select_bitcast_fusion
  78.1 3.6 %collective-permute-done.7 = bf16[64,2048]{1,0:T(8,128)(2,1)} collective-permute-done((bf16[64,2048]{1,0:T(8,128)(2,1)S(1)}, bf16[64,2048]{1,0:T(8,128)(2,1)}, u32[]{:S(2)}, u32[]{:S(2)}) %collective-permute-start.7) | collective-permute-done | bytes 262176 | tf_op jit(solution)/shard_map/ppermute | solution.py:24
  81.6 0.7 collective-permute-done.10
  82.3 1.1 add_convert_fusion.6
  83.6 11.9 %all_to_all.21 = bf16[16,64,128]{2,1,0:T(8,128)(2,1)S(1)} all-to-all(bf16[16,64,128]{2,1,0:T(8,128)(2,1)S(1)} %reshape.40), channel_id=1, replica_groups={{0,8,16,24,32,40,48,56,64,72,80,88,96,104,112,120},{1,9,17,25,33,41,49,..., dimensions={0} | all-to-all | bytes 524288 | tf_op jit(solution)/shard_map/all_to_all | solution.py:33
  95.6 2.5 %shard_map.98 = (bf16[128,2048]{1,0:T(8,128)(2,1)}, bf16[128,2048]{1,0:T(8,128)(2,1)S(1)}, f32[2,128]{1,0:T(2,128)}, bf16[128,2048]{1,0:T(8,128)(2,1)S(1)}) custom-call(s32[1,1]{1,0:T(1,128)S(6)} %copy.10.length_ref, s32[1]{0:T(128)} %bitcast.section_ref, bf16[128,2048]{1,0:T(8,128)(2,1)S(1)} %bitcast.35, f32[2,128]{1,0:T(2,128)S(1)} %bitcast.38, ...), custom_call_target="tpu_custom_call" | custom-call | bytes 1048576 | tf_op jit(solution)/shard_map/pallas_call | solution.py:210
  98.4 23.3 %all_to_all.22 = bf16[32,64,128]{2,1,0:T(8,128)(2,1)S(1)} all-to-all(bf16[32,64,128]{2,1,0:T(8,128)(2,1)S(1)} %reshape.42), channel_id=1, replica_groups={{0,8,16,24,32,40,48,56,64,72,80,88,96,104,112,120,4,12,20,28,36,44,52,6..., dimensions={0} | all-to-all | bytes 1048576 | tf_op jit(solution)/shard_map/all_to_all | solution.py:46
  122.0 3.2 %collective-permute-start.14 = (bf16[128,2048]{1,0:T(8,128)(2,1)S(1)}, bf16[128,2048]{1,0:T(8,128)(2,1)S(1)}, u32[]{:S(2)}, u32[]{:S(2)}) collective-permute-start(bf16[128,2048]{1,0:T(8,128)(2,1)S(1)} %reshape.43.refs_0_), channel_id=1, source_target_pairs={{0,7},{1,0},{2,1},{3,2},{4,3},{5,4},{6,5},{7,6},{8,15},{9,8},{10,9... | collective-permute-start | bytes 1572872 | tf_op jit(solution)/shard_map/ppermute | solution.py:24
  125.2 2.2 %copy-done.2 = bf16[1,2048,1024]{2,1,0:T(8,128)(2,1)S(1)} copy-done((bf16[1,2048,1024]{2,1,0:T(8,128)(2,1)S(1)}, bf16[1,2048,1024]{2,1,0:T(8,128)(2,1)}, u32[]{:S(2)}) %copy-start.2) | copy-done | bytes 4194328
  127.4 2.2 %copy-done.4 = bf16[1,1024,2048]{2,1,0:T(8,128)(2,1)S(1)} copy-done((bf16[1,1024,2048]{2,1,0:T(8,128)(2,1)S(1)}, bf16[1,1024,2048]{2,1,0:T(8,128)(2,1)}, u32[]{:S(2)}) %copy-start.4) | copy-done | bytes 4194328
  129.6 3.4 %shard_map.99 = (bf16[64,2048]{1,0:T(8,128)(2,1)S(1)}, bf16[64,2048]{1,0:T(8,128)(2,1)S(1)}) custom-call(s32[3]{0:T(128)S(1)} %pad_add_fusion.flip_ref, bf16[128,2048]{1,0:T(8,128)(2,1)S(1)} %reshape.43.refs_0_, bf16[128,1024]{1,0:T(8,128)(2,1)S(1)} %get-tuple-element.43.refs_1_, bf16[2048,1024]{1,0:T(8,128)(2,1)S(1)} %bitcast.25, ...), custom_call_target="tpu_custom_call" | custom-call | flops 1073741824 | bytes 1048576 | tf_op jit(solution)/shard_map/pallas_call | solution.py:210
  133.1 4.8 %collective-permute-done.13.refs_0_ = bf16[128,2048]{1,0:T(8,128)(2,1)S(1)} collective-permute-done((bf16[128,2048]{1,0:T(8,128)(2,1)S(1)}, bf16[128,2048]{1,0:T(8,128)(2,1)S(1)}, u32[]{:S(2)}, u32[]{:S(2)}) %collective-permute-start.13) | collective-permute-done | bytes 524320 | tf_op jit(solution)/shard_map/ppermute | solution.py:24
  138.1 3.5 %collective-permute-start.17 = (bf16[64,2048]{1,0:T(8,128)(2,1)S(1)}, bf16[64,2048]{1,0:T(8,128)(2,1)S(1)}, u32[]{:S(2)}, u32[]{:S(2)}) collective-permute-start(bf16[64,2048]{1,0:T(8,128)(2,1)S(1)} %slice_select_fusion), channel_id=1, source_target_pairs={{0,7},{1,0},{2,1},{3,2},{4,3},{5,4},{6,5},{7,6},{8,15},{9,8},{10,9... | collective-permute-start | bytes 786440 | tf_op jit(solution)/shard_map/ppermute | solution.py:24
  141.7 2.9 %shard_map.100 = (bf16[64,2048]{1,0:T(8,128)(2,1)S(1)}, bf16[64,2048]{1,0:T(8,128)(2,1)S(1)}, bf16[64,2048]{1,0:T(8,128)(2,1)S(1)}, bf16[64,2048]{1,0:T(8,128)(2,1)S(1)}) custom-call(s32[3]{0:T(128)S(1)} %pad_add_fusion.flip_ref, bf16[128,2048]{1,0:T(8,128)(2,1)S(1)} %collective-permute-done.13.refs_0_, ...), custom_call_target="tpu_custom_call" | custom-call | flops 2147483648 | bytes 1048576 | tf_op jit(solution)/shard_map/pallas_call | solution.py:210
  144.8 3.2 %collective-permute-start.20 = (bf16[64,2048]{1,0:T(8,128)(2,1)S(1)}, bf16[64,2048]{1,0:T(8,128)(2,1)S(1)}, u32[]{:S(2)}, u32[]{:S(2)}) collective-permute-start(bf16[64,2048]{1,0:T(8,128)(2,1)S(1)} %get-tuple-element.51), channel_id=1, source_target_pairs={{0,7},{1,0},{2,1},{3,2},{4,3},{5,4},{6,5},{7,6},{8,15},{9,8},{10,9... | collective-permute-start | bytes 786440 | tf_op jit(solution)/shard_map/ppermute | solution.py:24
  148.0 3.4 %shard_map.101 = (bf16[64,2048]{1,0:T(8,128)(2,1)S(1)}, bf16[64,2048]{1,0:T(8,128)(2,1)S(1)}) custom-call(s32[3]{0:T(128)S(1)} %pad_add_fusion.flip_ref, bf16[64,2048]{1,0:T(8,128)(2,1)S(1)} %collective-permute-done.16.refs_0_, bf16[64,2048]{1,0:T(8,128)(2,1)S(1)} %collective-permute-done.17.refs_1_, bf16[128,1024]{1,0:T(8,128)(2,1)S(1)} %get-tuple-element.48.refs_2_, ...), custom_call_target="tpu_custom_call" | custom-call | flops 1073741824 | bytes 1048576 | tf_op jit(solution)/shard_map/pallas_call | solution.py:210
  151.4 0.9 collective-permute-done.15
  152.6 3.3 %collective-permute-start.21 = (bf16[64,2048]{1,0:T(8,128)(2,1)S(1)}, bf16[64,2048]{1,0:T(8,128)(2,1)S(1)}, u32[]{:S(2)}, u32[]{:S(2)}) collective-permute-start(bf16[64,2048]{1,0:T(8,128)(2,1)S(1)} %add_convert_fusion.2), channel_id=1, source_target_pairs={{0,7},{1,0},{2,1},{3,2},{4,3},{5,4},{6,5},{7,6},{8,15},{9,8},{10,9... | collective-permute-start | bytes 786440 | tf_op jit(solution)/shard_map/ppermute | solution.py:24
  155.9 4.2 %collective-permute-done.18 = bf16[64,2048]{1,0:T(8,128)(2,1)S(1)} collective-permute-done((bf16[64,2048]{1,0:T(8,128)(2,1)S(1)}, bf16[64,2048]{1,0:T(8,128)(2,1)S(1)}, u32[]{:S(2)}, u32[]{:S(2)}) %collective-permute-start.18) | collective-permute-done | bytes 262176 | tf_op jit(solution)/shard_map/ppermute | solution.py:24
  160.3 3.3 %collective-permute-start.22 = (bf16[64,2048]{1,0:T(8,128)(2,1)S(1)}, bf16[64,2048]{1,0:T(8,128)(2,1)S(1)}, u32[]{:S(2)}, u32[]{:S(2)}) collective-permute-start(bf16[64,2048]{1,0:T(8,128)(2,1)S(1)} %add_convert_fusion.1), channel_id=1, source_target_pairs={{0,7},{1,0},{2,1},{3,2},{4,3},{5,4},{6,5},{7,6},{8,15},{9,8},{10,9... | collective-permute-start | bytes 786440 | tf_op jit(solution)/shard_map/ppermute | solution.py:24
  163.6 4.2 %collective-permute-done.19 = bf16[64,2048]{1,0:T(8,128)(2,1)S(1)} collective-permute-done((bf16[64,2048]{1,0:T(8,128)(2,1)S(1)}, bf16[64,2048]{1,0:T(8,128)(2,1)S(1)}, u32[]{:S(2)}, u32[]{:S(2)}) %collective-permute-start.19) | collective-permute-done | bytes 262176 | tf_op jit(solution)/shard_map/ppermute | solution.py:24
  168.0 12.0 %all_to_all.23 = bf16[16,64,128]{2,1,0:T(8,128)(2,1)S(1)} all-to-all(bf16[16,64,128]{2,1,0:T(8,128)(2,1)S(1)} %reshape.44), channel_id=1, replica_groups={{0,8,16,24,32,40,48,56,64,72,80,88,96,104,112,120},{1,9,17,25,33,41,49,..., dimensions={0} | all-to-all | bytes 524288 | tf_op jit(solution)/shard_map/all_to_all | solution.py:33
  180.2 1.6 shard_map.102
  (57 shorter events, 2.7 us)
Async XLA Ops:
  1.3 1.0 copy-start.5
  2.3 0.7 copy-start.7
  33.4 17.9 %collective-permute-start.1 = (bf16[128,2048]{1,0:T(8,128)(2,1)S(1)}, bf16[128,2048]{1,0:T(8,128)(2,1)S(1)}, u32[]{:S(2)}, u32[]{:S(2)}) collective-permute-start(bf16[128,2048]{1,0:T(8,128)(2,1)S(1)} %reshape.39.refs_0_), channel_id=1, source_target_pairs={{0,1},{1,2},{2,3},{3,4},{4,5},{5,6},{6,7},{7,0},{8,9},{9,10},{10,1... | collective-permute-start | bytes 1572872 | tf_op jit(solution)/shard_map/ppermute | solution.py:24
  39.0 14.9 %collective-permute-start.2 = (bf16[128,2048]{1,0:T(8,128)(2,1)S(1)}, bf16[128,2048]{1,0:T(8,128)(2,1)S(1)}, u32[]{:S(2)}, u32[]{:S(2)}) collective-permute-start(bf16[128,2048]{1,0:T(8,128)(2,1)S(1)} %reshape.39.refs_0_), channel_id=1, source_target_pairs={{0,7},{1,0},{2,1},{3,2},{4,3},{5,4},{6,5},{7,6},{8,15},{9,8},{10,9... | collective-permute-start | bytes 1572872 | tf_op jit(solution)/shard_map/ppermute | solution.py:24
  39.0 2.2 %copy-start = (bf16[1,2048,1024]{2,1,0:T(8,128)(2,1)S(1)}, bf16[1,2048,1024]{2,1,0:T(8,128)(2,1)}, u32[]{:S(2)}) copy-start(bf16[1,2048,1024]{2,1,0:T(8,128)(2,1)} %param.11) | copy-start | bytes 12582916
  41.2 2.2 %copy-start.3 = (bf16[1,1024,2048]{2,1,0:T(8,128)(2,1)S(1)}, bf16[1,1024,2048]{2,1,0:T(8,128)(2,1)}, u32[]{:S(2)}) copy-start(bf16[1,1024,2048]{2,1,0:T(8,128)(2,1)} %param.12) | copy-start | bytes 12582916
  43.4 11.4 %copy-start.1 = (bf16[1,2048,1024]{2,1,0:T(8,128)(2,1)S(1)}, bf16[1,2048,1024]{2,1,0:T(8,128)(2,1)}, u32[]{:S(2)}) copy-start(bf16[1,2048,1024]{2,1,0:T(8,128)(2,1)} %param.11) | copy-start | bytes 12582916
  45.3 12.4 %collective-permute-start = (bf16[64,2048]{1,0:T(8,128)(2,1)S(1)}, bf16[64,2048]{1,0:T(8,128)(2,1)S(1)}, u32[]{:S(2)}, u32[]{:S(2)}) collective-permute-start(bf16[64,2048]{1,0:T(8,128)(2,1)S(1)} %get-tuple-element.33), channel_id=1, source_target_pairs={{0,1},{1,2},{2,3},{3,4},{4,5},{5,6},{6,7},{7,0},{8,9},{9,10},{10,1... | collective-permute-start | bytes 786440 | tf_op jit(solution)/shard_map/ppermute | solution.py:24
  51.3 11.2 %collective-permute-start.4 = (bf16[64,2048]{1,0:T(8,128)(2,1)S(1)}, bf16[64,2048]{1,0:T(8,128)(2,1)S(1)}, u32[]{:S(2)}, u32[]{:S(2)}) collective-permute-start(bf16[64,2048]{1,0:T(8,128)(2,1)S(1)} %slice_select_fusion.3), channel_id=1, source_target_pairs={{0,1},{1,2},{2,3},{3,4},{4,5},{5,6},{6,7},{7,0},{8,9},{9,10},{10,1... | collective-permute-start | bytes 786440 | tf_op jit(solution)/shard_map/ppermute | solution.py:24
  53.9 9.1 %collective-permute-start.5 = (bf16[64,2048]{1,0:T(8,128)(2,1)S(1)}, bf16[64,2048]{1,0:T(8,128)(2,1)S(1)}, u32[]{:S(2)}, u32[]{:S(2)}) collective-permute-start(bf16[64,2048]{1,0:T(8,128)(2,1)S(1)} %slice_select_fusion.2), channel_id=1, source_target_pairs={{0,7},{1,0},{2,1},{3,2},{4,3},{5,4},{6,5},{7,6},{8,15},{9,8},{10,9... | collective-permute-start | bytes 786440 | tf_op jit(solution)/shard_map/ppermute | solution.py:24
  57.8 8.1 %collective-permute-start.3 = (bf16[64,2048]{1,0:T(8,128)(2,1)S(1)}, bf16[64,2048]{1,0:T(8,128)(2,1)S(1)}, u32[]{:S(2)}, u32[]{:S(2)}) collective-permute-start(bf16[64,2048]{1,0:T(8,128)(2,1)S(1)} %add_convert_fusion.11), channel_id=1, source_target_pairs={{0,1},{1,2},{2,3},{3,4},{4,5},{5,6},{6,7},{7,0},{8,9},{9,10},{10,1... | collective-permute-start | bytes 786440 | tf_op jit(solution)/shard_map/ppermute | solution.py:24
  59.5 17.8 %copy-start.9 = (bf16[2,128,1024]{2,1,0:T(8,128)(2,1)S(1)}, bf16[2,128,1024]{2,1,0:T(8,128)(2,1)}, u32[]{:S(2)}) copy-start(bf16[2,128,1024]{2,1,0:T(8,128)(2,1)} %param.13) | copy-start | bytes 1572868
  59.5 9.2 %collective-permute-start.8 = (bf16[64,2048]{1,0:T(8,128)(2,1)S(1)}, bf16[64,2048]{1,0:T(8,128)(2,1)S(1)}, u32[]{:S(2)}, u32[]{:S(2)}) collective-permute-start(bf16[64,2048]{1,0:T(8,128)(2,1)S(1)} %get-tuple-element.37), channel_id=1, source_target_pairs={{0,7},{1,0},{2,1},{3,2},{4,3},{5,4},{6,5},{7,6},{8,15},{9,8},{10,9... | collective-permute-start | bytes 786440 | tf_op jit(solution)/shard_map/ppermute | solution.py:24
  64.9 30.7 %copy-start.6 = (bf16[1,128,2048]{2,1,0:T(8,128)(2,1)S(1)}, bf16[1,128,2048]{2,1,0:T(8,128)(2,1)}, u32[]{:S(2)}) copy-start(bf16[1,128,2048]{2,1,0:T(8,128)(2,1)} %param.7) | copy-start | bytes 1572868
  64.9 30.7 %copy-start.8 = (f32[1,128,2]{1,2,0:T(2,128)S(1)}, f32[1,128,2]{1,2,0:T(2,128)}, u32[]{:S(2)}) copy-start(f32[1,128,2]{1,2,0:T(2,128)} %param.9) | copy-start | bytes 3076
  66.0 7.8 %collective-permute-start.6 = (bf16[64,2048]{1,0:T(8,128)(2,1)S(1)}, bf16[64,2048]{1,0:T(8,128)(2,1)S(1)}, u32[]{:S(2)}, u32[]{:S(2)}) collective-permute-start(bf16[64,2048]{1,0:T(8,128)(2,1)S(1)} %add_convert_fusion.10), channel_id=1, source_target_pairs={{0,1},{1,2},{2,3},{3,4},{4,5},{5,6},{6,7},{7,0},{8,9},{9,10},{10,1... | collective-permute-start | bytes 786440 | tf_op jit(solution)/shard_map/ppermute | solution.py:24
  68.8 7.0 %collective-permute-start.9 = (bf16[64,2048]{1,0:T(8,128)(2,1)S(1)}, bf16[64,2048]{1,0:T(8,128)(2,1)S(1)}, u32[]{:S(2)}, u32[]{:S(2)}) collective-permute-start(bf16[64,2048]{1,0:T(8,128)(2,1)S(1)} %add_convert_fusion.8), channel_id=1, source_target_pairs={{0,7},{1,0},{2,1},{3,2},{4,3},{5,4},{6,5},{7,6},{8,15},{9,8},{10,9... | collective-permute-start | bytes 786440 | tf_op jit(solution)/shard_map/ppermute | solution.py:24
  73.9 7.8 %collective-permute-start.7 = (bf16[64,2048]{1,0:T(8,128)(2,1)S(1)}, bf16[64,2048]{1,0:T(8,128)(2,1)}, u32[]{:S(2)}, u32[]{:S(2)}) collective-permute-start(bf16[64,2048]{1,0:T(8,128)(2,1)S(1)} %add_convert_fusion.9), channel_id=1, source_target_pairs={{0,1},{1,2},{2,3},{3,4},{4,5},{5,6},{6,7},{7,0},{8,9},{9,10},{10,1... | collective-permute-start | bytes 786440 | tf_op jit(solution)/shard_map/ppermute | solution.py:24
  75.8 6.6 %collective-permute-start.10 = (bf16[64,2048]{1,0:T(8,128)(2,1)S(1)}, bf16[64,2048]{1,0:T(8,128)(2,1)}, u32[]{:S(2)}, u32[]{:S(2)}) collective-permute-start(bf16[64,2048]{1,0:T(8,128)(2,1)S(1)} %add_convert_fusion.7), channel_id=1, source_target_pairs={{0,7},{1,0},{2,1},{3,2},{4,3},{5,4},{6,5},{7,6},{8,15},{9,8},{10,9... | collective-permute-start | bytes 786440 | tf_op jit(solution)/shard_map/ppermute | solution.py:24
  78.1 17.5 %collective-permute-start.11 = (bf16[128,1024]{1,0:T(8,128)(2,1)}, bf16[128,1024]{1,0:T(8,128)(2,1)S(1)}, u32[]{:S(2)}, u32[]{:S(2)}) collective-permute-start(bf16[128,1024]{1,0:T(8,128)(2,1)} %get-tuple-element.55), channel_id=1, source_target_pairs={{0,128},{128,0},{1,129},{129,1},{2,130},{130,2},{3,131},{131,3},{4... | collective-permute-start | bytes 786440 | tf_op jit(solution)/shard_map/ppermute | solution.py:232
  121.9 16.1 %collective-permute-start.13 = (bf16[128,2048]{1,0:T(8,128)(2,1)S(1)}, bf16[128,2048]{1,0:T(8,128)(2,1)S(1)}, u32[]{:S(2)}, u32[]{:S(2)}) collective-permute-start(bf16[128,2048]{1,0:T(8,128)(2,1)S(1)} %reshape.43.refs_0_), channel_id=1, source_target_pairs={{0,1},{1,2},{2,3},{3,4},{4,5},{5,6},{6,7},{7,0},{8,9},{9,10},{10,1... | collective-permute-start | bytes 1572872 | tf_op jit(solution)/shard_map/ppermute | solution.py:24
  122.0 16.1 %collective-permute-start.14 = (bf16[128,2048]{1,0:T(8,128)(2,1)S(1)}, bf16[128,2048]{1,0:T(8,128)(2,1)S(1)}, u32[]{:S(2)}, u32[]{:S(2)}) collective-permute-start(bf16[128,2048]{1,0:T(8,128)(2,1)S(1)} %reshape.43.refs_0_), channel_id=1, source_target_pairs={{0,7},{1,0},{2,1},{3,2},{4,3},{5,4},{6,5},{7,6},{8,15},{9,8},{10,9... | collective-permute-start | bytes 1572872 | tf_op jit(solution)/shard_map/ppermute | solution.py:24
  125.2 2.2 %copy-start.2 = (bf16[1,2048,1024]{2,1,0:T(8,128)(2,1)S(1)}, bf16[1,2048,1024]{2,1,0:T(8,128)(2,1)}, u32[]{:S(2)}) copy-start(bf16[1,2048,1024]{2,1,0:T(8,128)(2,1)} %param.11) | copy-start | bytes 12582916
  127.4 2.2 %copy-start.4 = (bf16[1,1024,2048]{2,1,0:T(8,128)(2,1)S(1)}, bf16[1,1024,2048]{2,1,0:T(8,128)(2,1)}, u32[]{:S(2)}) copy-start(bf16[1,1024,2048]{2,1,0:T(8,128)(2,1)} %param.12) | copy-start | bytes 12582916
  133.1 11.5 %collective-permute-start.12 = (bf16[64,2048]{1,0:T(8,128)(2,1)S(1)}, bf16[64,2048]{1,0:T(8,128)(2,1)S(1)}, u32[]{:S(2)}, u32[]{:S(2)}) collective-permute-start(bf16[64,2048]{1,0:T(8,128)(2,1)S(1)} %get-tuple-element.45), channel_id=1, source_target_pairs={{0,1},{1,2},{2,3},{3,4},{4,5},{5,6},{6,7},{7,0},{8,9},{9,10},{10,1... | collective-permute-start | bytes 786440 | tf_op jit(solution)/shard_map/ppermute | solution.py:24
  138.0 10.0 %collective-permute-start.16 = (bf16[64,2048]{1,0:T(8,128)(2,1)S(1)}, bf16[64,2048]{1,0:T(8,128)(2,1)S(1)}, u32[]{:S(2)}, u32[]{:S(2)}) collective-permute-start(bf16[64,2048]{1,0:T(8,128)(2,1)S(1)} %slice_select_fusion.1), channel_id=1, source_target_pairs={{0,1},{1,2},{2,3},{3,4},{4,5},{5,6},{6,7},{7,0},{8,9},{9,10},{10,1... | collective-permute-start | bytes 786440 | tf_op jit(solution)/shard_map/ppermute | solution.py:24
  138.1 9.9 %collective-permute-start.17 = (bf16[64,2048]{1,0:T(8,128)(2,1)S(1)}, bf16[64,2048]{1,0:T(8,128)(2,1)S(1)}, u32[]{:S(2)}, u32[]{:S(2)}) collective-permute-start(bf16[64,2048]{1,0:T(8,128)(2,1)S(1)} %slice_select_fusion), channel_id=1, source_target_pairs={{0,7},{1,0},{2,1},{3,2},{4,3},{5,4},{6,5},{7,6},{8,15},{9,8},{10,9... | collective-permute-start | bytes 786440 | tf_op jit(solution)/shard_map/ppermute | solution.py:24
  144.7 7.7 %collective-permute-start.15 = (bf16[64,2048]{1,0:T(8,128)(2,1)S(1)}, bf16[64,2048]{1,0:T(8,128)(2,1)S(1)}, u32[]{:S(2)}, u32[]{:S(2)}) collective-permute-start(bf16[64,2048]{1,0:T(8,128)(2,1)S(1)} %add_convert_fusion.5), channel_id=1, source_target_pairs={{0,1},{1,2},{2,3},{3,4},{4,5},{5,6},{6,7},{7,0},{8,9},{9,10},{10,1... | collective-permute-start | bytes 786440 | tf_op jit(solution)/shard_map/ppermute | solution.py:24
  144.8 7.7 %collective-permute-start.20 = (bf16[64,2048]{1,0:T(8,128)(2,1)S(1)}, bf16[64,2048]{1,0:T(8,128)(2,1)S(1)}, u32[]{:S(2)}, u32[]{:S(2)}) collective-permute-start(bf16[64,2048]{1,0:T(8,128)(2,1)S(1)} %get-tuple-element.51), channel_id=1, source_target_pairs={{0,7},{1,0},{2,1},{3,2},{4,3},{5,4},{6,5},{7,6},{8,15},{9,8},{10,9... | collective-permute-start | bytes 786440 | tf_op jit(solution)/shard_map/ppermute | solution.py:24
  152.4 7.7 %collective-permute-start.18 = (bf16[64,2048]{1,0:T(8,128)(2,1)S(1)}, bf16[64,2048]{1,0:T(8,128)(2,1)S(1)}, u32[]{:S(2)}, u32[]{:S(2)}) collective-permute-start(bf16[64,2048]{1,0:T(8,128)(2,1)S(1)} %add_convert_fusion.4), channel_id=1, source_target_pairs={{0,1},{1,2},{2,3},{3,4},{4,5},{5,6},{6,7},{7,0},{8,9},{9,10},{10,1... | collective-permute-start | bytes 786440 | tf_op jit(solution)/shard_map/ppermute | solution.py:24
  152.6 7.6 %collective-permute-start.21 = (bf16[64,2048]{1,0:T(8,128)(2,1)S(1)}, bf16[64,2048]{1,0:T(8,128)(2,1)S(1)}, u32[]{:S(2)}, u32[]{:S(2)}) collective-permute-start(bf16[64,2048]{1,0:T(8,128)(2,1)S(1)} %add_convert_fusion.2), channel_id=1, source_target_pairs={{0,7},{1,0},{2,1},{3,2},{4,3},{5,4},{6,5},{7,6},{8,15},{9,8},{10,9... | collective-permute-start | bytes 786440 | tf_op jit(solution)/shard_map/ppermute | solution.py:24
  160.1 7.7 %collective-permute-start.19 = (bf16[64,2048]{1,0:T(8,128)(2,1)S(1)}, bf16[64,2048]{1,0:T(8,128)(2,1)S(1)}, u32[]{:S(2)}, u32[]{:S(2)}) collective-permute-start(bf16[64,2048]{1,0:T(8,128)(2,1)S(1)} %add_convert_fusion.3), channel_id=1, source_target_pairs={{0,1},{1,2},{2,3},{3,4},{4,5},{5,6},{6,7},{7,0},{8,9},{9,10},{10,1... | collective-permute-start | bytes 786440 | tf_op jit(solution)/shard_map/ppermute | solution.py:24
  160.3 7.5 %collective-permute-start.22 = (bf16[64,2048]{1,0:T(8,128)(2,1)S(1)}, bf16[64,2048]{1,0:T(8,128)(2,1)S(1)}, u32[]{:S(2)}, u32[]{:S(2)}) collective-permute-start(bf16[64,2048]{1,0:T(8,128)(2,1)S(1)} %add_convert_fusion.1), channel_id=1, source_target_pairs={{0,7},{1,0},{2,1},{3,2},{4,3},{5,4},{6,5},{7,6},{8,15},{9,8},{10,9... | collective-permute-start | bytes 786440 | tf_op jit(solution)/shard_map/ppermute | solution.py:24

commit v2 on v1

--- a/solution.py
+++ b/solution.py
@@ -12,7 +12,7 @@
 LIVE = 16
 SLOTS = LIVE * CAP
 EPS = 1e-05
-COST = 4
+COST = 1
 BF = jnp.bfloat16
 F32 = jnp.float32
 VMEM_LIMIT = 16 * 2**20
@@ -54,9 +54,11 @@
     return jnp.where(flip, pair[half:], pair[:half])
 
 
-def exchange(rows, flips, expert):
+def exchange(rows, flips, expert, ahead=()):
     pair = swap_pair(rows)
     up, down = hop(pair, 1), hop(pair, -1)
+    if ahead:
+        up, *ahead = lax.optimization_barrier((up, *ahead))
     ((own, across),) = expert(0, [pair])
     sum_up = hop(across, 1)
     up_2, down_2 = hop(nearer(up, flips[1] == 1), 1), hop(nearer(down, flips[2] == 1), -1)
@@ -65,7 +67,8 @@
     low_2, high_2 = expert(2, [up_2, down_2])
     sum_up, sum_down = hop(plus(sum_up, high_2), 1), hop(plus(sum_down, low_2), -1)
     sum_up, sum_down = hop(plus(sum_up, high_1), 1), hop(plus(sum_down, low_1), -1)
-    return (own.astype(F32) + sum_up.astype(F32) + sum_down.astype(F32)).astype(BF)
+    total = own.astype(F32) + sum_up.astype(F32) + sum_down.astype(F32)
+    return total.astype(BF), ahead
 
 
 def plus(a, b):
@@ -229,7 +232,6 @@
 
     keep = jnp.where(section == 0, incoming[0], incoming[1])
     send = jnp.where(section == 0, incoming[1], incoming[0])
-    other = lax.ppermute(send, "section", [(0, 1), (1, 0)])
 
     rows, first, second = call(
         dispatch_kernel, [twice, table, table], 2, lengths, section_id, routes[0].T, source
@@ -266,7 +268,9 @@
     def backward(key, blocks):
         return run(backward_kernel, key, blocks, [acts[key], w_in, w_out], [])[1]
 
-    y = swap_plane(exchange(rows, flips, forward))
+    y, (keep, send) = exchange(rows, flips, forward, (keep, send))
+    other = lax.ppermute(send, "section", [(0, 1), (1, 0)])
+    y = swap_plane(y)
 
     result, upstream, gate_grad, grad_rows = call(
         middle_kernel,
@@ -283,7 +287,7 @@
         other,
     )
 
-    d_rows = swap_plane(exchange(grad_rows, flips, backward))
+    d_rows = swap_plane(exchange(grad_rows, flips, backward)[0])
 
     hidden_grad = call(final_kernel, wide, 0, source, upstream, first, second, d_rows)
     return (result[None], hidden_grad[None], gate_grad.T[None])

time: 182 us -> 181 us (level)
  transfers between devices with their start and end apart: 23 -> 23, of which waited for: 11 -> 11; matrix products, arithmetic and copies ran while one was open for 2% -> 1% of each run, Pallas kernels for 9% -> 9%
where the time goes in v2:
time: 181 us; the launch traced here: 180 us
  blocking collectives  76.1 us (42%)
  starting transfers between devices  38.4 us (21%)
  waiting for transfers between devices  30 us (17%)
  Pallas kernels  21.1 us (12%)
  local copies, waits for them, and re-layouts  11.9 us (7%)
    all_to_all x2, blocking collectives, swap_pair(): lax.all_to_all(packed, 'expert', split_axis=0, concat_axis=0, axis_index_...  52.8 us
    ppermute x22, starting transfers between devices, hop(): return lax.ppermute(value, 'expert', pairs)  38.4 us
    ppermute x22, waiting for transfers between devices, hop(): return lax.ppermute(value, 'expert', pairs)  30 us
    all_to_all x2, blocking collectives, swap_plane(): lax.all_to_all(packed, 'expert', split_axis=0, concat_axis=0, axis_index_...  23.3 us
    pallas_call x9, Pallas kernels, call(): pl.pallas_call(kernel, out_shape=outs, in_specs=[pl.BlockSpec(memory_spac...  21.1 us
    unnamed x20, local copies, waits for them, and re-layouts  10.5 us
  transfers between devices with their start and end apart: 23, of which 11 were waited for; matrix products, arithmetic and copies ran while one was open for 1% of the time, Pallas kernels for 9%

profile of v2, /device:TPU:8, one launch (start us, length us, event | category | flops | bytes accessed | tf_op | source)
XLA Modules:
  0.0 180.3 jit_solution(9297336222045605040)
XLA Ops:
  1.3 1.0 copy-done.5
  2.3 0.7 copy-done.7
  3.0 0.6 shard_map.94
  3.6 0.2 reshape.38
  3.8 29.4 %all_to_all.20 = bf16[32,64,128]{2,1,0:T(8,128)(2,1)S(1)} all-to-all(bf16[32,64,128]{2,1,0:T(8,128)(2,1)S(1)} %reshape.38), channel_id=1, replica_groups={{0,8,16,24,32,40,48,56,64,72,80,88,96,104,112,120,4,12,20,28,36,44,52,6..., dimensions={0} | all-to-all | bytes 1048576 | tf_op jit(solution)/shard_map/all_to_all | solution.py:46
  33.2 0.2 reshape.39.refs_0_
  33.4 5.5 %collective-permute-start.1 = (bf16[128,2048]{1,0:T(8,128)(2,1)S(1)}, bf16[128,2048]{1,0:T(8,128)(2,1)S(1)}, u32[]{:S(2)}, u32[]{:S(2)}) collective-permute-start(bf16[128,2048]{1,0:T(8,128)(2,1)S(1)} %reshape.39.refs_0_), channel_id=1, source_target_pairs={{0,1},{1,2},{2,3},{3,4},{4,5},{5,6},{6,7},{7,0},{8,9},{9,10},{10,1... | collective-permute-start | bytes 1572872 | tf_op jit(solution)/shard_map/ppermute | solution.py:24
  39.1 2.2 %copy-done = bf16[1,2048,1024]{2,1,0:T(8,128)(2,1)S(1)} copy-done((bf16[1,2048,1024]{2,1,0:T(8,128)(2,1)S(1)}, bf16[1,2048,1024]{2,1,0:T(8,128)(2,1)}, u32[]{:S(2)}) %copy-start) | copy-done | bytes 4194328
  41.3 2.2 %copy-done.3 = bf16[1,1024,2048]{2,1,0:T(8,128)(2,1)S(1)} copy-done((bf16[1,1024,2048]{2,1,0:T(8,128)(2,1)S(1)}, bf16[1,1024,2048]{2,1,0:T(8,128)(2,1)}, u32[]{:S(2)}) %copy-start.3) | copy-done | bytes 4194328
  43.5 1.9 %shard_map.95 = (bf16[128,1024]{1,0:T(8,128)(2,1)S(1)}, bf16[64,2048]{1,0:T(8,128)(2,1)S(1)}, bf16[64,2048]{1,0:T(8,128)(2,1)S(1)}) custom-call(s32[3]{0:T(128)S(1)} %pad_add_fusion.flip_ref, bf16[128,2048]{1,0:T(8,128)(2,1)S(1)} %reshape.39.refs_0_, bf16[2048,1024]{1,0:T(8,128)(2,1)S(1)} %bitcast.22, bf16[1024,2048]{1,0:T(8,128)(2,1)S(1)} %bitcast.28), custom_call_target="tpu_custom_call" | custom-call | flops 268435456 | bytes 1048576 | tf_op jit(solution)/shard_map/pallas_call | solution.py:213
  45.4 2.1 %collective-permute-start = (bf16[64,2048]{1,0:T(8,128)(2,1)S(1)}, bf16[64,2048]{1,0:T(8,128)(2,1)S(1)}, u32[]{:S(2)}, u32[]{:S(2)}) collective-permute-start(bf16[64,2048]{1,0:T(8,128)(2,1)S(1)} %get-tuple-element.36), channel_id=1, source_target_pairs={{0,1},{1,2},{2,3},{3,4},{4,5},{5,6},{6,7},{7,0},{8,9},{9,10},{10,1... | collective-permute-start | bytes 786440 | tf_op jit(solution)/shard_map/ppermute | solution.py:24
  47.5 3.8 %collective-permute-done.1.refs_0_ = bf16[128,2048]{1,0:T(8,128)(2,1)S(1)} collective-permute-done((bf16[128,2048]{1,0:T(8,128)(2,1)S(1)}, bf16[128,2048]{1,0:T(8,128)(2,1)S(1)}, u32[]{:S(2)}, u32[]{:S(2)}) %collective-permute-start.1) | collective-permute-done | bytes 524320 | tf_op jit(solution)/shard_map/ppermute | solution.py:24
  51.3 2.6 %collective-permute-start.4 = (bf16[64,2048]{1,0:T(8,128)(2,1)S(1)}, bf16[64,2048]{1,0:T(8,128)(2,1)S(1)}, u32[]{:S(2)}, u32[]{:S(2)}) collective-permute-start(bf16[64,2048]{1,0:T(8,128)(2,1)S(1)} %slice_select_fusion.3), channel_id=1, source_target_pairs={{0,1},{1,2},{2,3},{3,4},{4,5},{5,6},{6,7},{7,0},{8,9},{9,10},{10,1... | collective-permute-start | bytes 786440 | tf_op jit(solution)/shard_map/ppermute | solution.py:24
  53.9 0.8 collective-permute-start.5
  54.8 2.9 %shard_map.96 = (bf16[256,1024]{1,0:T(8,128)(2,1)S(1)}, bf16[64,2048]{1,0:T(8,128)(2,1)S(1)}, bf16[64,2048]{1,0:T(8,128)(2,1)S(1)}, bf16[64,2048]{1,0:T(8,128)(2,1)S(1)}, bf16[64,2048]{1,0:T(8,128)(2,1)S(1)}) custom-call(s32[3]{0:T(128)S(1)} %pad_add_fusion.flip_ref, bf16[128,2048]{1,0:T(8,128)(2,1)S(1)} %collective-permute-done.1.refs_0_, ...), custom_call_target="tpu_custom_call" | custom-call | flops 536870912 | bytes 1048576 | tf_op jit(solution)/shard_map/pallas_call | solution.py:213
  57.8 1.7 collective-permute-start.3
  59.6 1.6 collective-permute-start.8
  61.1 1.4 collective-permute-done.4.refs_0_
  62.5 0.5 collective-permute-done.5.refs_1_
  63.0 1.9 %shard_map.97 = (bf16[128,1024]{1,0:T(8,128)(2,1)S(1)}, bf16[64,2048]{1,0:T(8,128)(2,1)S(1)}, bf16[64,2048]{1,0:T(8,128)(2,1)S(1)}) custom-call(s32[3]{0:T(128)S(1)} %pad_add_fusion.flip_ref, bf16[64,2048]{1,0:T(8,128)(2,1)S(1)} %collective-permute-done.4.refs_0_, bf16[64,2048]{1,0:T(8,128)(2,1)S(1)} %collective-permute-done.5.refs_1_, ...), custom_call_target="tpu_custom_call" | custom-call | flops 268435456 | bytes 1048576 | tf_op jit(solution)/shard_map/pallas_call | solution.py:213
  64.9 0.9 collective-permute-done.3
  66.0 2.7 %collective-permute-start.6 = (bf16[64,2048]{1,0:T(8,128)(2,1)S(1)}, bf16[64,2048]{1,0:T(8,128)(2,1)S(1)}, u32[]{:S(2)}, u32[]{:S(2)}) collective-permute-start(bf16[64,2048]{1,0:T(8,128)(2,1)S(1)} %add_convert_fusion.10), channel_id=1, source_target_pairs={{0,1},{1,2},{2,3},{3,4},{4,5},{5,6},{6,7},{7,0},{8,9},{9,10},{10,1... | collective-permute-start | bytes 786440 | tf_op jit(solution)/shard_map/ppermute | solution.py:24
  68.8 0.8 collective-permute-start.9
  69.6 4.2 %collective-permute-done.6 = bf16[64,2048]{1,0:T(8,128)(2,1)S(1)} collective-permute-done((bf16[64,2048]{1,0:T(8,128)(2,1)S(1)}, bf16[64,2048]{1,0:T(8,128)(2,1)S(1)}, u32[]{:S(2)}, u32[]{:S(2)}) %collective-permute-start.6) | collective-permute-done | bytes 262176 | tf_op jit(solution)/shard_map/ppermute | solution.py:24
  73.9 1.9 %collective-permute-start.7 = (bf16[64,2048]{1,0:T(8,128)(2,1)S(1)}, bf16[64,2048]{1,0:T(8,128)(2,1)S(1)}, u32[]{:S(2)}, u32[]{:S(2)}) collective-permute-start(bf16[64,2048]{1,0:T(8,128)(2,1)S(1)} %add_convert_fusion.9), channel_id=1, source_target_pairs={{0,1},{1,2},{2,3},{3,4},{4,5},{5,6},{6,7},{7,0},{8,9},{9,10},{10,1... | collective-permute-start | bytes 786440 | tf_op jit(solution)/shard_map/ppermute | solution.py:24
  75.8 1.5 collective-permute-start.10
  77.3 4.2 %collective-permute-done.7 = bf16[64,2048]{1,0:T(8,128)(2,1)S(1)} collective-permute-done((bf16[64,2048]{1,0:T(8,128)(2,1)S(1)}, bf16[64,2048]{1,0:T(8,128)(2,1)S(1)}, u32[]{:S(2)}, u32[]{:S(2)}) %collective-permute-start.7) | collective-permute-done | bytes 262176 | tf_op jit(solution)/shard_map/ppermute | solution.py:24
  81.5 0.7 collective-permute-done.10
  82.5 11.9 %all_to_all.21 = bf16[16,64,128]{2,1,0:T(8,128)(2,1)S(1)} all-to-all(bf16[16,64,128]{2,1,0:T(8,128)(2,1)S(1)} %reshape.40), channel_id=1, replica_groups={{0,8,16,24,32,40,48,56,64,72,80,88,96,104,112,120},{1,9,17,25,33,41,49,..., dimensions={0} | all-to-all | bytes 524288 | tf_op jit(solution)/shard_map/all_to_all | solution.py:33
  94.5 2.5 %shard_map.98 = (bf16[128,2048]{1,0:T(8,128)(2,1)}, bf16[128,2048]{1,0:T(8,128)(2,1)S(1)}, f32[2,128]{1,0:T(2,128)}, bf16[128,2048]{1,0:T(8,128)(2,1)S(1)}) custom-call(s32[1,1]{1,0:T(1,128)S(6)} %copy.10.length_ref, s32[1]{0:T(128)} %bitcast.section_ref, bf16[128,2048]{1,0:T(8,128)(2,1)S(1)} %bitcast.35, f32[2,128]{1,0:T(2,128)S(1)} %bitcast.38, ...), custom_call_target="tpu_custom_call" | custom-call | bytes 1048576 | tf_op jit(solution)/shard_map/pallas_call | solution.py:213
  97.0 0.2 reshape.42
  97.3 23.5 %all_to_all.22 = bf16[32,64,128]{2,1,0:T(8,128)(2,1)S(1)} all-to-all(bf16[32,64,128]{2,1,0:T(8,128)(2,1)S(1)} %reshape.42), channel_id=1, replica_groups={{0,8,16,24,32,40,48,56,64,72,80,88,96,104,112,120,4,12,20,28,36,44,52,6..., dimensions={0} | all-to-all | bytes 1048576 | tf_op jit(solution)/shard_map/all_to_all | solution.py:46
  121.0 3.2 %collective-permute-start.14 = (bf16[128,2048]{1,0:T(8,128)(2,1)S(1)}, bf16[128,2048]{1,0:T(8,128)(2,1)S(1)}, u32[]{:S(2)}, u32[]{:S(2)}) collective-permute-start(bf16[128,2048]{1,0:T(8,128)(2,1)S(1)} %reshape.43.refs_0_), channel_id=1, source_target_pairs={{0,7},{1,0},{2,1},{3,2},{4,3},{5,4},{6,5},{7,6},{8,15},{9,8},{10,9... | collective-permute-start | bytes 1572872 | tf_op jit(solution)/shard_map/ppermute | solution.py:24
  124.3 2.2 %copy-done.2 = bf16[1,2048,1024]{2,1,0:T(8,128)(2,1)S(1)} copy-done((bf16[1,2048,1024]{2,1,0:T(8,128)(2,1)S(1)}, bf16[1,2048,1024]{2,1,0:T(8,128)(2,1)}, u32[]{:S(2)}) %copy-start.2) | copy-done | bytes 4194328
  126.5 2.2 %copy-done.4 = bf16[1,1024,2048]{2,1,0:T(8,128)(2,1)S(1)} copy-done((bf16[1,1024,2048]{2,1,0:T(8,128)(2,1)S(1)}, bf16[1,1024,2048]{2,1,0:T(8,128)(2,1)}, u32[]{:S(2)}) %copy-start.4) | copy-done | bytes 4194328
  128.6 3.4 %shard_map.99 = (bf16[64,2048]{1,0:T(8,128)(2,1)S(1)}, bf16[64,2048]{1,0:T(8,128)(2,1)S(1)}) custom-call(s32[3]{0:T(128)S(1)} %pad_add_fusion.flip_ref, bf16[128,2048]{1,0:T(8,128)(2,1)S(1)} %reshape.43.refs_0_, bf16[128,1024]{1,0:T(8,128)(2,1)S(1)} %get-tuple-element.49.refs_1_, bf16[2048,1024]{1,0:T(8,128)(2,1)S(1)} %bitcast.25, ...), custom_call_target="tpu_custom_call" | custom-call | flops 268435456 | bytes 1048576 | tf_op jit(solution)/shard_map/pallas_call | solution.py:213
  132.2 4.9 %collective-permute-done.13.refs_0_ = bf16[128,2048]{1,0:T(8,128)(2,1)S(1)} collective-permute-done((bf16[128,2048]{1,0:T(8,128)(2,1)S(1)}, bf16[128,2048]{1,0:T(8,128)(2,1)S(1)}, u32[]{:S(2)}, u32[]{:S(2)}) %collective-permute-start.13) | collective-permute-done | bytes 524320 | tf_op jit(solution)/shard_map/ppermute | solution.py:24
  137.3 3.5 %collective-permute-start.17 = (bf16[64,2048]{1,0:T(8,128)(2,1)S(1)}, bf16[64,2048]{1,0:T(8,128)(2,1)S(1)}, u32[]{:S(2)}, u32[]{:S(2)}) collective-permute-start(bf16[64,2048]{1,0:T(8,128)(2,1)S(1)} %slice_select_fusion), channel_id=1, source_target_pairs={{0,7},{1,0},{2,1},{3,2},{4,3},{5,4},{6,5},{7,6},{8,15},{9,8},{10,9... | collective-permute-start | bytes 786440 | tf_op jit(solution)/shard_map/ppermute | solution.py:24
  140.8 2.9 %shard_map.100 = (bf16[64,2048]{1,0:T(8,128)(2,1)S(1)}, bf16[64,2048]{1,0:T(8,128)(2,1)S(1)}, bf16[64,2048]{1,0:T(8,128)(2,1)S(1)}, bf16[64,2048]{1,0:T(8,128)(2,1)S(1)}) custom-call(s32[3]{0:T(128)S(1)} %pad_add_fusion.flip_ref, bf16[128,2048]{1,0:T(8,128)(2,1)S(1)} %collective-permute-done.13.refs_0_, ...), custom_call_target="tpu_custom_call" | custom-call | flops 536870912 | bytes 1048576 | tf_op jit(solution)/shard_map/pallas_call | solution.py:213
  143.9 3.2 %collective-permute-start.20 = (bf16[64,2048]{1,0:T(8,128)(2,1)S(1)}, bf16[64,2048]{1,0:T(8,128)(2,1)S(1)}, u32[]{:S(2)}, u32[]{:S(2)}) collective-permute-start(bf16[64,2048]{1,0:T(8,128)(2,1)S(1)} %get-tuple-element.57), channel_id=1, source_target_pairs={{0,7},{1,0},{2,1},{3,2},{4,3},{5,4},{6,5},{7,6},{8,15},{9,8},{10,9... | collective-permute-start | bytes 786440 | tf_op jit(solution)/shard_map/ppermute | solution.py:24
  147.1 3.4 %shard_map.101 = (bf16[64,2048]{1,0:T(8,128)(2,1)S(1)}, bf16[64,2048]{1,0:T(8,128)(2,1)S(1)}) custom-call(s32[3]{0:T(128)S(1)} %pad_add_fusion.flip_ref, bf16[64,2048]{1,0:T(8,128)(2,1)S(1)} %collective-permute-done.16.refs_0_, bf16[64,2048]{1,0:T(8,128)(2,1)S(1)} %collective-permute-done.17.refs_1_, bf16[128,1024]{1,0:T(8,128)(2,1)S(1)} %get-tuple-element.54.refs_2_, ...), custom_call_target="tpu_custom_call" | custom-call | flops 268435456 | bytes 1048576 | tf_op jit(solution)/shard_map/pallas_call | solution.py:213
  150.6 0.9 collective-permute-done.15
  151.7 3.3 %collective-permute-start.21 = (bf16[64,2048]{1,0:T(8,128)(2,1)S(1)}, bf16[64,2048]{1,0:T(8,128)(2,1)S(1)}, u32[]{:S(2)}, u32[]{:S(2)}) collective-permute-start(bf16[64,2048]{1,0:T(8,128)(2,1)S(1)} %add_convert_fusion.2), channel_id=1, source_target_pairs={{0,7},{1,0},{2,1},{3,2},{4,3},{5,4},{6,5},{7,6},{8,15},{9,8},{10,9... | collective-permute-start | bytes 786440 | tf_op jit(solution)/shard_map/ppermute | solution.py:24
  155.0 4.2 %collective-permute-done.18 = bf16[64,2048]{1,0:T(8,128)(2,1)S(1)} collective-permute-done((bf16[64,2048]{1,0:T(8,128)(2,1)S(1)}, bf16[64,2048]{1,0:T(8,128)(2,1)S(1)}, u32[]{:S(2)}, u32[]{:S(2)}) %collective-permute-start.18) | collective-permute-done | bytes 262176 | tf_op jit(solution)/shard_map/ppermute | solution.py:24
  159.5 3.3 %collective-permute-start.22 = (bf16[64,2048]{1,0:T(8,128)(2,1)S(1)}, bf16[64,2048]{1,0:T(8,128)(2,1)S(1)}, u32[]{:S(2)}, u32[]{:S(2)}) collective-permute-start(bf16[64,2048]{1,0:T(8,128)(2,1)S(1)} %add_convert_fusion.1), channel_id=1, source_target_pairs={{0,7},{1,0},{2,1},{3,2},{4,3},{5,4},{6,5},{7,6},{8,15},{9,8},{10,9... | collective-permute-start | bytes 786440 | tf_op jit(solution)/shard_map/ppermute | solution.py:24
  162.8 4.2 %collective-permute-done.19 = bf16[64,2048]{1,0:T(8,128)(2,1)S(1)} collective-permute-done((bf16[64,2048]{1,0:T(8,128)(2,1)S(1)}, bf16[64,2048]{1,0:T(8,128)(2,1)S(1)}, u32[]{:S(2)}, u32[]{:S(2)}) %collective-permute-start.19) | collective-permute-done | bytes 262176 | tf_op jit(solution)/shard_map/ppermute | solution.py:24
  167.2 11.4 %all_to_all.23 = bf16[16,64,128]{2,1,0:T(8,128)(2,1)S(1)} all-to-all(bf16[16,64,128]{2,1,0:T(8,128)(2,1)S(1)} %reshape.44), channel_id=1, replica_groups={{0,8,16,24,32,40,48,56,64,72,80,88,96,104,112,120},{1,9,17,25,33,41,49,..., dimensions={0} | all-to-all | bytes 524288 | tf_op jit(solution)/shard_map/all_to_all | solution.py:33
  178.7 1.6 shard_map.102
  (57 shorter events, 2.5 us)
Async XLA Ops:
  1.3 1.0 copy-start.5
  2.3 0.7 copy-start.7
  3.0 35.9 %copy-start.9 = (bf16[2,128,1024]{2,1,0:T(8,128)(2,1)S(1)}, bf16[2,128,1024]{2,1,0:T(8,128)(2,1)}, u32[]{:S(2)}) copy-start(bf16[2,128,1024]{2,1,0:T(8,128)(2,1)} %param.13) | copy-start | bytes 1572868
  33.4 17.9 %collective-permute-start.1 = (bf16[128,2048]{1,0:T(8,128)(2,1)S(1)}, bf16[128,2048]{1,0:T(8,128)(2,1)S(1)}, u32[]{:S(2)}, u32[]{:S(2)}) collective-permute-start(bf16[128,2048]{1,0:T(8,128)(2,1)S(1)} %reshape.39.refs_0_), channel_id=1, source_target_pairs={{0,1},{1,2},{2,3},{3,4},{4,5},{5,6},{6,7},{7,0},{8,9},{9,10},{10,1... | collective-permute-start | bytes 1572872 | tf_op jit(solution)/shard_map/ppermute | solution.py:24
  39.0 14.9 %collective-permute-start.2 = (bf16[128,2048]{1,0:T(8,128)(2,1)S(1)}, bf16[128,2048]{1,0:T(8,128)(2,1)S(1)}, u32[]{:S(2)}, u32[]{:S(2)}) collective-permute-start(bf16[128,2048]{1,0:T(8,128)(2,1)S(1)} %reshape.39.refs_0_), channel_id=1, source_target_pairs={{0,7},{1,0},{2,1},{3,2},{4,3},{5,4},{6,5},{7,6},{8,15},{9,8},{10,9... | collective-permute-start | bytes 1572872 | tf_op jit(solution)/shard_map/ppermute | solution.py:24
  39.1 2.2 %copy-start = (bf16[1,2048,1024]{2,1,0:T(8,128)(2,1)S(1)}, bf16[1,2048,1024]{2,1,0:T(8,128)(2,1)}, u32[]{:S(2)}) copy-start(bf16[1,2048,1024]{2,1,0:T(8,128)(2,1)} %param.11) | copy-start | bytes 12582916
  41.3 2.2 %copy-start.3 = (bf16[1,1024,2048]{2,1,0:T(8,128)(2,1)S(1)}, bf16[1,1024,2048]{2,1,0:T(8,128)(2,1)}, u32[]{:S(2)}) copy-start(bf16[1,1024,2048]{2,1,0:T(8,128)(2,1)} %param.12) | copy-start | bytes 12582916
  43.5 11.2 %copy-start.1 = (bf16[1,2048,1024]{2,1,0:T(8,128)(2,1)S(1)}, bf16[1,2048,1024]{2,1,0:T(8,128)(2,1)}, u32[]{:S(2)}) copy-start(bf16[1,2048,1024]{2,1,0:T(8,128)(2,1)} %param.11) | copy-start | bytes 12582916
  45.4 12.3 %collective-permute-start = (bf16[64,2048]{1,0:T(8,128)(2,1)S(1)}, bf16[64,2048]{1,0:T(8,128)(2,1)S(1)}, u32[]{:S(2)}, u32[]{:S(2)}) collective-permute-start(bf16[64,2048]{1,0:T(8,128)(2,1)S(1)} %get-tuple-element.36), channel_id=1, source_target_pairs={{0,1},{1,2},{2,3},{3,4},{4,5},{5,6},{6,7},{7,0},{8,9},{9,10},{10,1... | collective-permute-start | bytes 786440 | tf_op jit(solution)/shard_map/ppermute | solution.py:24
  51.3 11.2 %collective-permute-start.4 = (bf16[64,2048]{1,0:T(8,128)(2,1)S(1)}, bf16[64,2048]{1,0:T(8,128)(2,1)S(1)}, u32[]{:S(2)}, u32[]{:S(2)}) collective-permute-start(bf16[64,2048]{1,0:T(8,128)(2,1)S(1)} %slice_select_fusion.3), channel_id=1, source_target_pairs={{0,1},{1,2},{2,3},{3,4},{4,5},{5,6},{6,7},{7,0},{8,9},{9,10},{10,1... | collective-permute-start | bytes 786440 | tf_op jit(solution)/shard_map/ppermute | solution.py:24
  53.9 9.1 %collective-permute-start.5 = (bf16[64,2048]{1,0:T(8,128)(2,1)S(1)}, bf16[64,2048]{1,0:T(8,128)(2,1)S(1)}, u32[]{:S(2)}, u32[]{:S(2)}) collective-permute-start(bf16[64,2048]{1,0:T(8,128)(2,1)S(1)} %slice_select_fusion.2), channel_id=1, source_target_pairs={{0,7},{1,0},{2,1},{3,2},{4,3},{5,4},{6,5},{7,6},{8,15},{9,8},{10,9... | collective-permute-start | bytes 786440 | tf_op jit(solution)/shard_map/ppermute | solution.py:24
  57.8 8.1 %collective-permute-start.3 = (bf16[64,2048]{1,0:T(8,128)(2,1)S(1)}, bf16[64,2048]{1,0:T(8,128)(2,1)S(1)}, u32[]{:S(2)}, u32[]{:S(2)}) collective-permute-start(bf16[64,2048]{1,0:T(8,128)(2,1)S(1)} %add_convert_fusion.11), channel_id=1, source_target_pairs={{0,1},{1,2},{2,3},{3,4},{4,5},{5,6},{6,7},{7,0},{8,9},{9,10},{10,1... | collective-permute-start | bytes 786440 | tf_op jit(solution)/shard_map/ppermute | solution.py:24
  59.6 9.2 %collective-permute-start.8 = (bf16[64,2048]{1,0:T(8,128)(2,1)S(1)}, bf16[64,2048]{1,0:T(8,128)(2,1)S(1)}, u32[]{:S(2)}, u32[]{:S(2)}) collective-permute-start(bf16[64,2048]{1,0:T(8,128)(2,1)S(1)} %get-tuple-element.41), channel_id=1, source_target_pairs={{0,7},{1,0},{2,1},{3,2},{4,3},{5,4},{6,5},{7,6},{8,15},{9,8},{10,9... | collective-permute-start | bytes 786440 | tf_op jit(solution)/shard_map/ppermute | solution.py:24
  64.9 29.6 %copy-start.6 = (bf16[1,128,2048]{2,1,0:T(8,128)(2,1)S(1)}, bf16[1,128,2048]{2,1,0:T(8,128)(2,1)}, u32[]{:S(2)}) copy-start(bf16[1,128,2048]{2,1,0:T(8,128)(2,1)} %param.7) | copy-start | bytes 1572868
  64.9 29.6 %copy-start.8 = (f32[1,128,2]{1,2,0:T(2,128)S(1)}, f32[1,128,2]{1,2,0:T(2,128)}, u32[]{:S(2)}) copy-start(f32[1,128,2]{1,2,0:T(2,128)} %param.9) | copy-start | bytes 3076
  66.0 7.8 %collective-permute-start.6 = (bf16[64,2048]{1,0:T(8,128)(2,1)S(1)}, bf16[64,2048]{1,0:T(8,128)(2,1)S(1)}, u32[]{:S(2)}, u32[]{:S(2)}) collective-permute-start(bf16[64,2048]{1,0:T(8,128)(2,1)S(1)} %add_convert_fusion.10), channel_id=1, source_target_pairs={{0,1},{1,2},{2,3},{3,4},{4,5},{5,6},{6,7},{7,0},{8,9},{9,10},{10,1... | collective-permute-start | bytes 786440 | tf_op jit(solution)/shard_map/ppermute | solution.py:24
  68.8 7.0 %collective-permute-start.9 = (bf16[64,2048]{1,0:T(8,128)(2,1)S(1)}, bf16[64,2048]{1,0:T(8,128)(2,1)S(1)}, u32[]{:S(2)}, u32[]{:S(2)}) collective-permute-start(bf16[64,2048]{1,0:T(8,128)(2,1)S(1)} %add_convert_fusion.8), channel_id=1, source_target_pairs={{0,7},{1,0},{2,1},{3,2},{4,3},{5,4},{6,5},{7,6},{8,15},{9,8},{10,9... | collective-permute-start | bytes 786440 | tf_op jit(solution)/shard_map/ppermute | solution.py:24
  73.9 7.7 %collective-permute-start.7 = (bf16[64,2048]{1,0:T(8,128)(2,1)S(1)}, bf16[64,2048]{1,0:T(8,128)(2,1)S(1)}, u32[]{:S(2)}, u32[]{:S(2)}) collective-permute-start(bf16[64,2048]{1,0:T(8,128)(2,1)S(1)} %add_convert_fusion.9), channel_id=1, source_target_pairs={{0,1},{1,2},{2,3},{3,4},{4,5},{5,6},{6,7},{7,0},{8,9},{9,10},{10,1... | collective-permute-start | bytes 786440 | tf_op jit(solution)/shard_map/ppermute | solution.py:24
  75.8 6.5 %collective-permute-start.10 = (bf16[64,2048]{1,0:T(8,128)(2,1)S(1)}, bf16[64,2048]{1,0:T(8,128)(2,1)S(1)}, u32[]{:S(2)}, u32[]{:S(2)}) collective-permute-start(bf16[64,2048]{1,0:T(8,128)(2,1)S(1)} %add_convert_fusion.7), channel_id=1, source_target_pairs={{0,7},{1,0},{2,1},{3,2},{4,3},{5,4},{6,5},{7,6},{8,15},{9,8},{10,9... | collective-permute-start | bytes 786440 | tf_op jit(solution)/shard_map/ppermute | solution.py:24
  77.3 17.1 %collective-permute-start.11 = (bf16[128,1024]{1,0:T(8,128)(2,1)S(1)}, bf16[128,1024]{1,0:T(8,128)(2,1)S(1)}, u32[]{:S(2)}, u32[]{:S(2)}) collective-permute-start(bf16[128,1024]{1,0:T(8,128)(2,1)S(1)} %get-tuple-element.45), channel_id=1, source_target_pairs={{0,128},{128,0},{1,129},{129,1},{2,130},{130,2},{3,131},{131,3},{4... | collective-permute-start | bytes 786440 | tf_op jit(solution)/shard_map/ppermute | solution.py:272
  121.0 16.1 %collective-permute-start.13 = (bf16[128,2048]{1,0:T(8,128)(2,1)S(1)}, bf16[128,2048]{1,0:T(8,128)(2,1)S(1)}, u32[]{:S(2)}, u32[]{:S(2)}) collective-permute-start(bf16[128,2048]{1,0:T(8,128)(2,1)S(1)} %reshape.43.refs_0_), channel_id=1, source_target_pairs={{0,1},{1,2},{2,3},{3,4},{4,5},{5,6},{6,7},{7,0},{8,9},{9,10},{10,1... | collective-permute-start | bytes 1572872 | tf_op jit(solution)/shard_map/ppermute | solution.py:24
  121.0 16.2 %collective-permute-start.14 = (bf16[128,2048]{1,0:T(8,128)(2,1)S(1)}, bf16[128,2048]{1,0:T(8,128)(2,1)S(1)}, u32[]{:S(2)}, u32[]{:S(2)}) collective-permute-start(bf16[128,2048]{1,0:T(8,128)(2,1)S(1)} %reshape.43.refs_0_), channel_id=1, source_target_pairs={{0,7},{1,0},{2,1},{3,2},{4,3},{5,4},{6,5},{7,6},{8,15},{9,8},{10,9... | collective-permute-start | bytes 1572872 | tf_op jit(solution)/shard_map/ppermute | solution.py:24
  124.3 2.2 %copy-start.2 = (bf16[1,2048,1024]{2,1,0:T(8,128)(2,1)S(1)}, bf16[1,2048,1024]{2,1,0:T(8,128)(2,1)}, u32[]{:S(2)}) copy-start(bf16[1,2048,1024]{2,1,0:T(8,128)(2,1)} %param.11) | copy-start | bytes 12582916
  126.5 2.2 %copy-start.4 = (bf16[1,1024,2048]{2,1,0:T(8,128)(2,1)S(1)}, bf16[1,1024,2048]{2,1,0:T(8,128)(2,1)}, u32[]{:S(2)}) copy-start(bf16[1,1024,2048]{2,1,0:T(8,128)(2,1)} %param.12) | copy-start | bytes 12582916
  132.1 11.6 %collective-permute-start.12 = (bf16[64,2048]{1,0:T(8,128)(2,1)S(1)}, bf16[64,2048]{1,0:T(8,128)(2,1)S(1)}, u32[]{:S(2)}, u32[]{:S(2)}) collective-permute-start(bf16[64,2048]{1,0:T(8,128)(2,1)S(1)} %get-tuple-element.51), channel_id=1, source_target_pairs={{0,1},{1,2},{2,3},{3,4},{4,5},{5,6},{6,7},{7,0},{8,9},{9,10},{10,1... | collective-permute-start | bytes 786440 | tf_op jit(solution)/shard_map/ppermute | solution.py:24
  137.1 10.0 %collective-permute-start.16 = (bf16[64,2048]{1,0:T(8,128)(2,1)S(1)}, bf16[64,2048]{1,0:T(8,128)(2,1)S(1)}, u32[]{:S(2)}, u32[]{:S(2)}) collective-permute-start(bf16[64,2048]{1,0:T(8,128)(2,1)S(1)} %slice_select_fusion.1), channel_id=1, source_target_pairs={{0,1},{1,2},{2,3},{3,4},{4,5},{5,6},{6,7},{7,0},{8,9},{9,10},{10,1... | collective-permute-start | bytes 786440 | tf_op jit(solution)/shard_map/ppermute | solution.py:24
  137.3 9.9 %collective-permute-start.17 = (bf16[64,2048]{1,0:T(8,128)(2,1)S(1)}, bf16[64,2048]{1,0:T(8,128)(2,1)S(1)}, u32[]{:S(2)}, u32[]{:S(2)}) collective-permute-start(bf16[64,2048]{1,0:T(8,128)(2,1)S(1)} %slice_select_fusion), channel_id=1, source_target_pairs={{0,7},{1,0},{2,1},{3,2},{4,3},{5,4},{6,5},{7,6},{8,15},{9,8},{10,9... | collective-permute-start | bytes 786440 | tf_op jit(solution)/shard_map/ppermute | solution.py:24
  143.8 7.7 %collective-permute-start.15 = (bf16[64,2048]{1,0:T(8,128)(2,1)S(1)}, bf16[64,2048]{1,0:T(8,128)(2,1)S(1)}, u32[]{:S(2)}, u32[]{:S(2)}) collective-permute-start(bf16[64,2048]{1,0:T(8,128)(2,1)S(1)} %add_convert_fusion.5), channel_id=1, source_target_pairs={{0,1},{1,2},{2,3},{3,4},{4,5},{5,6},{6,7},{7,0},{8,9},{9,10},{10,1... | collective-permute-start | bytes 786440 | tf_op jit(solution)/shard_map/ppermute | solution.py:24
  143.9 7.8 %collective-permute-start.20 = (bf16[64,2048]{1,0:T(8,128)(2,1)S(1)}, bf16[64,2048]{1,0:T(8,128)(2,1)S(1)}, u32[]{:S(2)}, u32[]{:S(2)}) collective-permute-start(bf16[64,2048]{1,0:T(8,128)(2,1)S(1)} %get-tuple-element.57), channel_id=1, source_target_pairs={{0,7},{1,0},{2,1},{3,2},{4,3},{5,4},{6,5},{7,6},{8,15},{9,8},{10,9... | collective-permute-start | bytes 786440 | tf_op jit(solution)/shard_map/ppermute | solution.py:24
  151.6 7.7 %collective-permute-start.18 = (bf16[64,2048]{1,0:T(8,128)(2,1)S(1)}, bf16[64,2048]{1,0:T(8,128)(2,1)S(1)}, u32[]{:S(2)}, u32[]{:S(2)}) collective-permute-start(bf16[64,2048]{1,0:T(8,128)(2,1)S(1)} %add_convert_fusion.4), channel_id=1, source_target_pairs={{0,1},{1,2},{2,3},{3,4},{4,5},{5,6},{6,7},{7,0},{8,9},{9,10},{10,1... | collective-permute-start | bytes 786440 | tf_op jit(solution)/shard_map/ppermute | solution.py:24
  151.7 7.7 %collective-permute-start.21 = (bf16[64,2048]{1,0:T(8,128)(2,1)S(1)}, bf16[64,2048]{1,0:T(8,128)(2,1)S(1)}, u32[]{:S(2)}, u32[]{:S(2)}) collective-permute-start(bf16[64,2048]{1,0:T(8,128)(2,1)S(1)} %add_convert_fusion.2), channel_id=1, source_target_pairs={{0,7},{1,0},{2,1},{3,2},{4,3},{5,4},{6,5},{7,6},{8,15},{9,8},{10,9... | collective-permute-start | bytes 786440 | tf_op jit(solution)/shard_map/ppermute | solution.py:24
  159.3 7.7 %collective-permute-start.19 = (bf16[64,2048]{1,0:T(8,128)(2,1)S(1)}, bf16[64,2048]{1,0:T(8,128)(2,1)S(1)}, u32[]{:S(2)}, u32[]{:S(2)}) collective-permute-start(bf16[64,2048]{1,0:T(8,128)(2,1)S(1)} %add_convert_fusion.3), channel_id=1, source_target_pairs={{0,1},{1,2},{2,3},{3,4},{4,5},{5,6},{6,7},{7,0},{8,9},{9,10},{10,1... | collective-permute-start | bytes 786440 | tf_op jit(solution)/shard_map/ppermute | solution.py:24
  159.5 7.5 %collective-permute-start.22 = (bf16[64,2048]{1,0:T(8,128)(2,1)S(1)}, bf16[64,2048]{1,0:T(8,128)(2,1)S(1)}, u32[]{:S(2)}, u32[]{:S(2)}) collective-permute-start(bf16[64,2048]{1,0:T(8,128)(2,1)S(1)} %add_convert_fusion.1), channel_id=1, source_target_pairs={{0,7},{1,0},{2,1},{3,2},{4,3},{5,4},{6,5},{7,6},{8,15},{9,8},{10,9... | collective-permute-start | bytes 786440 | tf_op jit(solution)/shard_map/ppermute | solution.py:24

commit v3 on v2

--- a/solution.py
+++ b/solution.py
@@ -20,8 +20,12 @@
 
 def hop(value, step):
     n = lax.axis_size("expert")
-    pairs = [(i, i // SPLIT * SPLIT + (i + step) % SPLIT) for i in range(n)]
-    return lax.ppermute(value, "expert", pairs)
+    pairs = []
+    for i in range(n):
+        column = i // SPLIT * SPLIT
+        pairs.append((i, column + (i + step) % SPLIT))
+        pairs.append((n + i, n + column + (i - step) % SPLIT))
+    return lax.ppermute(value, ("section", "expert"), pairs)
 
 
 def swap_plane(rows):
@@ -239,7 +243,9 @@
 
     hidden_units = w_in.shape[1]
     plane = lax.axis_index("expert") % SPLIT
-    flips = jnp.stack([(plane + d) % SPLIT // (SPLIT // 2) for d in (0, -1, 1)]).astype(jnp.int32)
+    turn = jnp.where(section == 0, 1, -1)
+    flips = jnp.stack([(plane + d * turn) % SPLIT // (SPLIT // 2) for d in (0, -1, 1)])
+    flips = flips.astype(jnp.int32)
     acts = {}
 
     def run(kernel, key, blocks, extra, outs):

time: 181 us -> 182 us (level)
  starting transfers between devices: 38.4 us -> 42.7 us
  waiting for transfers between devices: 30 us -> 27.9 us
    ppermute x22, starting transfers between devices: 38.4 us -> 42.7 us  [hop(): return lax.ppermute(value, ('section', 'expert'), pairs)]
    all_to_all x2, blocking collectives: 52.8 us -> 50.5 us  [swap_pair(): lax.all_to_all(packed, 'expert', split_axis=0, concat_axis=0, axis_index_...]
    ppermute x22, waiting for transfers between devices: 30 us -> 27.9 us  [hop(): return lax.ppermute(value, ('section', 'expert'), pairs)]
  transfers between devices with their start and end apart: 23 -> 23, of which waited for: 11 -> 16; matrix products, arithmetic and copies ran while one was open for 1% -> 1% of each run, Pallas kernels for 9% -> 9%
where the time goes in v3:
time: 182 us; the launch traced here: 181 us
  blocking collectives  74.3 us (41%)
  starting transfers between devices  42.7 us (23%)
  waiting for transfers between devices  27.9 us (15%)
  Pallas kernels  21.2 us (12%)
  local copies, waits for them, and re-layouts  11.9 us (7%)
    all_to_all x2, blocking collectives, swap_pair(): lax.all_to_all(packed, 'expert', split_axis=0, concat_axis=0, axis_index_...  50.5 us
    ppermute x22, starting transfers between devices, hop(): return lax.ppermute(value, ('section', 'expert'), pairs)  42.7 us
    ppermute x22, waiting for transfers between devices, hop(): return lax.ppermute(value, ('section', 'expert'), pairs)  27.9 us
    all_to_all x2, blocking collectives, swap_plane(): lax.all_to_all(packed, 'expert', split_axis=0, concat_axis=0, axis_index_...  23.8 us
    pallas_call x9, Pallas kernels, call(): pl.pallas_call(kernel, out_shape=outs, in_specs=[pl.BlockSpec(memory_spac...  21.2 us
    unnamed x20, local copies, waits for them, and re-layouts  10.5 us
  transfers between devices with their start and end apart: 23, of which 16 were waited for; matrix products, arithmetic and copies ran while one was open for 1% of the time, Pallas kernels for 9%

profile of v3, /device:TPU:8, one launch (start us, length us, event | category | flops | bytes accessed | tf_op | source)
XLA Modules:
  0.0 180.7 jit_solution(16534360304983881153)
XLA Ops:
  1.3 1.0 copy-done.5
  2.3 0.7 copy-done.7
  3.0 0.6 shard_map.94
  3.8 29.4 %all_to_all.20 = bf16[32,64,128]{2,1,0:T(8,128)(2,1)S(1)} all-to-all(bf16[32,64,128]{2,1,0:T(8,128)(2,1)S(1)} %reshape.38), channel_id=1, replica_groups={{0,8,16,24,32,40,48,56,64,72,80,88,96,104,112,120,4,12,20,28,36,44,52,6..., dimensions={0} | all-to-all | bytes 1048576 | tf_op jit(solution)/shard_map/all_to_all | solution.py:50
  33.4 5.6 %collective-permute-start.1 = (bf16[128,2048]{1,0:T(8,128)(2,1)S(1)}, bf16[128,2048]{1,0:T(8,128)(2,1)S(1)}, u32[]{:S(2)}, u32[]{:S(2)}) collective-permute-start(bf16[128,2048]{1,0:T(8,128)(2,1)S(1)} %reshape.39.refs_0_), channel_id=1, source_target_pairs={{0,1},{128,135},{1,2},{129,128},{2,3},{130,129},{3,4},{131,130},{4... | collective-permute-start | bytes 1572872 | tf_op jit(solution)/shard_map/ppermute | solution.py:28
  39.2 2.2 %copy-done = bf16[1,2048,1024]{2,1,0:T(8,128)(2,1)S(1)} copy-done((bf16[1,2048,1024]{2,1,0:T(8,128)(2,1)S(1)}, bf16[1,2048,1024]{2,1,0:T(8,128)(2,1)}, u32[]{:S(2)}) %copy-start) | copy-done | bytes 4194328
  41.4 2.2 %copy-done.3 = bf16[1,1024,2048]{2,1,0:T(8,128)(2,1)S(1)} copy-done((bf16[1,1024,2048]{2,1,0:T(8,128)(2,1)S(1)}, bf16[1,1024,2048]{2,1,0:T(8,128)(2,1)}, u32[]{:S(2)}) %copy-start.3) | copy-done | bytes 4194328
  43.6 1.9 %shard_map.95 = (bf16[128,1024]{1,0:T(8,128)(2,1)S(1)}, bf16[64,2048]{1,0:T(8,128)(2,1)S(1)}, bf16[64,2048]{1,0:T(8,128)(2,1)S(1)}) custom-call(s32[3]{0:T(128)S(1)} %pad_add_fusion.flip_ref, bf16[128,2048]{1,0:T(8,128)(2,1)S(1)} %reshape.39.refs_0_, bf16[2048,1024]{1,0:T(8,128)(2,1)S(1)} %bitcast.22, bf16[1024,2048]{1,0:T(8,128)(2,1)S(1)} %bitcast.28), custom_call_target="tpu_custom_call" | custom-call | flops 268435456 | bytes 1048576 | tf_op jit(solution)/shard_map/pallas_call | solution.py:217
  45.5 2.1 %collective-permute-start = (bf16[64,2048]{1,0:T(8,128)(2,1)S(1)}, bf16[64,2048]{1,0:T(8,128)(2,1)S(1)}, u32[]{:S(2)}, u32[]{:S(2)}) collective-permute-start(bf16[64,2048]{1,0:T(8,128)(2,1)S(1)} %get-tuple-element.36), channel_id=1, source_target_pairs={{0,1},{128,135},{1,2},{129,128},{2,3},{130,129},{3,4},{131,130},{4... | collective-permute-start | bytes 786440 | tf_op jit(solution)/shard_map/ppermute | solution.py:28
  47.6 1.7 collective-permute-done.1.refs_0_
  49.3 2.6 %collective-permute-start.4 = (bf16[64,2048]{1,0:T(8,128)(2,1)S(1)}, bf16[64,2048]{1,0:T(8,128)(2,1)S(1)}, u32[]{:S(2)}, u32[]{:S(2)}) collective-permute-start(bf16[64,2048]{1,0:T(8,128)(2,1)S(1)} %slice_select_fusion.3), channel_id=1, source_target_pairs={{0,1},{128,135},{1,2},{129,128},{2,3},{130,129},{3,4},{131,130},{4... | collective-permute-start | bytes 786440 | tf_op jit(solution)/shard_map/ppermute | solution.py:28
  51.9 0.9 collective-permute-done.2.refs_1_
  52.9 2.9 %shard_map.96 = (bf16[256,1024]{1,0:T(8,128)(2,1)S(1)}, bf16[64,2048]{1,0:T(8,128)(2,1)S(1)}, bf16[64,2048]{1,0:T(8,128)(2,1)S(1)}, bf16[64,2048]{1,0:T(8,128)(2,1)S(1)}, bf16[64,2048]{1,0:T(8,128)(2,1)S(1)}) custom-call(s32[3]{0:T(128)S(1)} %pad_add_fusion.flip_ref, bf16[128,2048]{1,0:T(8,128)(2,1)S(1)} %collective-permute-done.1.refs_0_, ...), custom_call_target="tpu_custom_call" | custom-call | flops 536870912 | bytes 1048576 | tf_op jit(solution)/shard_map/pallas_call | solution.py:217
  55.9 2.1 %collective-permute-start.3 = (bf16[64,2048]{1,0:T(8,128)(2,1)S(1)}, bf16[64,2048]{1,0:T(8,128)(2,1)S(1)}, u32[]{:S(2)}, u32[]{:S(2)}) collective-permute-start(bf16[64,2048]{1,0:T(8,128)(2,1)S(1)} %add_convert_fusion.11), channel_id=1, source_target_pairs={{0,1},{128,135},{1,2},{129,128},{2,3},{130,129},{3,4},{131,130},{4... | collective-permute-start | bytes 786440 | tf_op jit(solution)/shard_map/ppermute | solution.py:28
  58.0 1.2 collective-permute-start.8
  59.2 0.5 collective-permute-done.4.refs_0_
  59.7 1.8 collective-permute-done.5.refs_1_
  61.5 1.9 %shard_map.97 = (bf16[128,1024]{1,0:T(8,128)(2,1)S(1)}, bf16[64,2048]{1,0:T(8,128)(2,1)S(1)}, bf16[64,2048]{1,0:T(8,128)(2,1)S(1)}) custom-call(s32[3]{0:T(128)S(1)} %pad_add_fusion.flip_ref, bf16[64,2048]{1,0:T(8,128)(2,1)S(1)} %collective-permute-done.4.refs_0_, bf16[64,2048]{1,0:T(8,128)(2,1)S(1)} %collective-permute-done.5.refs_1_, ...), custom_call_target="tpu_custom_call" | custom-call | flops 268435456 | bytes 1048576 | tf_op jit(solution)/shard_map/pallas_call | solution.py:217
  63.4 1.0 collective-permute-done.3
  64.5 1.7 collective-permute-start.6
  66.2 1.9 %collective-permute-start.9 = (bf16[64,2048]{1,0:T(8,128)(2,1)S(1)}, bf16[64,2048]{1,0:T(8,128)(2,1)S(1)}, u32[]{:S(2)}, u32[]{:S(2)}) collective-permute-start(bf16[64,2048]{1,0:T(8,128)(2,1)S(1)} %add_convert_fusion.8), channel_id=1, source_target_pairs={{0,7},{128,129},{1,0},{129,130},{2,1},{130,131},{3,2},{131,132},{4... | collective-permute-start | bytes 786440 | tf_op jit(solution)/shard_map/ppermute | solution.py:28
  68.1 4.6 %collective-permute-done.6 = bf16[64,2048]{1,0:T(8,128)(2,1)S(1)} collective-permute-done((bf16[64,2048]{1,0:T(8,128)(2,1)S(1)}, bf16[64,2048]{1,0:T(8,128)(2,1)S(1)}, u32[]{:S(2)}, u32[]{:S(2)}) %collective-permute-start.6) | collective-permute-done | bytes 262176 | tf_op jit(solution)/shard_map/ppermute | solution.py:28
  72.9 2.5 %collective-permute-done.9 = bf16[64,2048]{1,0:T(8,128)(2,1)S(1)} collective-permute-done((bf16[64,2048]{1,0:T(8,128)(2,1)S(1)}, bf16[64,2048]{1,0:T(8,128)(2,1)S(1)}, u32[]{:S(2)}, u32[]{:S(2)}) %collective-permute-start.9) | collective-permute-done | bytes 262176 | tf_op jit(solution)/shard_map/ppermute | solution.py:28
  75.4 2.4 %collective-permute-start.10 = (bf16[64,2048]{1,0:T(8,128)(2,1)S(1)}, bf16[64,2048]{1,0:T(8,128)(2,1)S(1)}, u32[]{:S(2)}, u32[]{:S(2)}) collective-permute-start(bf16[64,2048]{1,0:T(8,128)(2,1)S(1)} %add_convert_fusion.7), channel_id=1, source_target_pairs={{0,7},{128,129},{1,0},{129,130},{2,1},{130,131},{3,2},{131,132},{4... | collective-permute-start | bytes 786440 | tf_op jit(solution)/shard_map/ppermute | solution.py:28
  77.8 2.7 %collective-permute-done.7 = bf16[64,2048]{1,0:T(8,128)(2,1)S(1)} collective-permute-done((bf16[64,2048]{1,0:T(8,128)(2,1)S(1)}, bf16[64,2048]{1,0:T(8,128)(2,1)S(1)}, u32[]{:S(2)}, u32[]{:S(2)}) %collective-permute-start.7) | collective-permute-done | bytes 262176 | tf_op jit(solution)/shard_map/ppermute | solution.py:28
  80.4 1.4 collective-permute-done.10
  82.1 12.0 %all_to_all.21 = bf16[16,64,128]{2,1,0:T(8,128)(2,1)S(1)} all-to-all(bf16[16,64,128]{2,1,0:T(8,128)(2,1)S(1)} %reshape.40), channel_id=1, replica_groups={{0,8,16,24,32,40,48,56,64,72,80,88,96,104,112,120},{1,9,17,25,33,41,49,..., dimensions={0} | all-to-all | bytes 524288 | tf_op jit(solution)/shard_map/all_to_all | solution.py:37
  94.2 2.5 %shard_map.98 = (bf16[128,2048]{1,0:T(8,128)(2,1)}, bf16[128,2048]{1,0:T(8,128)(2,1)S(1)}, f32[2,128]{1,0:T(2,128)}, bf16[128,2048]{1,0:T(8,128)(2,1)S(1)}) custom-call(s32[1,1]{1,0:T(1,128)S(6)} %copy.10.length_ref, s32[1]{0:T(128)} %bitcast.section_ref, bf16[128,2048]{1,0:T(8,128)(2,1)S(1)} %bitcast.35, f32[2,128]{1,0:T(2,128)S(1)} %bitcast.38, ...), custom_call_target="tpu_custom_call" | custom-call | bytes 1048576 | tf_op jit(solution)/shard_map/pallas_call | solution.py:217
  97.0 21.1 %all_to_all.22 = bf16[32,64,128]{2,1,0:T(8,128)(2,1)S(1)} all-to-all(bf16[32,64,128]{2,1,0:T(8,128)(2,1)S(1)} %reshape.42), channel_id=1, replica_groups={{0,8,16,24,32,40,48,56,64,72,80,88,96,104,112,120,4,12,20,28,36,44,52,6..., dimensions={0} | all-to-all | bytes 1048576 | tf_op jit(solution)/shard_map/all_to_all | solution.py:50
  118.4 5.7 %collective-permute-start.14 = (bf16[128,2048]{1,0:T(8,128)(2,1)S(1)}, bf16[128,2048]{1,0:T(8,128)(2,1)S(1)}, u32[]{:S(2)}, u32[]{:S(2)}) collective-permute-start(bf16[128,2048]{1,0:T(8,128)(2,1)S(1)} %reshape.43.refs_0_), channel_id=1, source_target_pairs={{0,7},{128,129},{1,0},{129,130},{2,1},{130,131},{3,2},{131,132},{4... | collective-permute-start | bytes 1572872 | tf_op jit(solution)/shard_map/ppermute | solution.py:28
  124.1 2.2 %copy-done.2 = bf16[1,2048,1024]{2,1,0:T(8,128)(2,1)S(1)} copy-done((bf16[1,2048,1024]{2,1,0:T(8,128)(2,1)S(1)}, bf16[1,2048,1024]{2,1,0:T(8,128)(2,1)}, u32[]{:S(2)}) %copy-start.2) | copy-done | bytes 4194328
  126.3 2.2 %copy-done.4 = bf16[1,1024,2048]{2,1,0:T(8,128)(2,1)S(1)} copy-done((bf16[1,1024,2048]{2,1,0:T(8,128)(2,1)S(1)}, bf16[1,1024,2048]{2,1,0:T(8,128)(2,1)}, u32[]{:S(2)}) %copy-start.4) | copy-done | bytes 4194328
  128.5 3.4 %shard_map.99 = (bf16[64,2048]{1,0:T(8,128)(2,1)S(1)}, bf16[64,2048]{1,0:T(8,128)(2,1)S(1)}) custom-call(s32[3]{0:T(128)S(1)} %pad_add_fusion.flip_ref, bf16[128,2048]{1,0:T(8,128)(2,1)S(1)} %reshape.43.refs_0_, bf16[128,1024]{1,0:T(8,128)(2,1)S(1)} %get-tuple-element.49.refs_1_, bf16[2048,1024]{1,0:T(8,128)(2,1)S(1)} %bitcast.25, ...), custom_call_target="tpu_custom_call" | custom-call | flops 268435456 | bytes 1048576 | tf_op jit(solution)/shard_map/pallas_call | solution.py:217
  131.9 0.3 collective-permute-start.12
  132.2 1.8 collective-permute-done.13.refs_0_
  134.0 2.7 %collective-permute-start.16 = (bf16[64,2048]{1,0:T(8,128)(2,1)S(1)}, bf16[64,2048]{1,0:T(8,128)(2,1)S(1)}, u32[]{:S(2)}, u32[]{:S(2)}) collective-permute-start(bf16[64,2048]{1,0:T(8,128)(2,1)S(1)} %slice_select_fusion.1), channel_id=1, source_target_pairs={{0,1},{128,135},{1,2},{129,128},{2,3},{130,129},{3,4},{131,130},{4... | collective-permute-start | bytes 786440 | tf_op jit(solution)/shard_map/ppermute | solution.py:28
  136.7 0.4 collective-permute-done.14.refs_1_
  137.2 3.3 %collective-permute-start.17 = (bf16[64,2048]{1,0:T(8,128)(2,1)S(1)}, bf16[64,2048]{1,0:T(8,128)(2,1)S(1)}, u32[]{:S(2)}, u32[]{:S(2)}) collective-permute-start(bf16[64,2048]{1,0:T(8,128)(2,1)S(1)} %slice_select_fusion), channel_id=1, source_target_pairs={{0,7},{128,129},{1,0},{129,130},{2,1},{130,131},{3,2},{131,132},{4... | collective-permute-start | bytes 786440 | tf_op jit(solution)/shard_map/ppermute | solution.py:28
  140.5 2.9 %shard_map.100 = (bf16[64,2048]{1,0:T(8,128)(2,1)S(1)}, bf16[64,2048]{1,0:T(8,128)(2,1)S(1)}, bf16[64,2048]{1,0:T(8,128)(2,1)S(1)}, bf16[64,2048]{1,0:T(8,128)(2,1)S(1)}) custom-call(s32[3]{0:T(128)S(1)} %pad_add_fusion.flip_ref, bf16[128,2048]{1,0:T(8,128)(2,1)S(1)} %collective-permute-done.13.refs_0_, ...), custom_call_target="tpu_custom_call" | custom-call | flops 536870912 | bytes 1048576 | tf_op jit(solution)/shard_map/pallas_call | solution.py:217
  143.6 3.2 %collective-permute-start.20 = (bf16[64,2048]{1,0:T(8,128)(2,1)S(1)}, bf16[64,2048]{1,0:T(8,128)(2,1)S(1)}, u32[]{:S(2)}, u32[]{:S(2)}) collective-permute-start(bf16[64,2048]{1,0:T(8,128)(2,1)S(1)} %get-tuple-element.57), channel_id=1, source_target_pairs={{0,7},{128,129},{1,0},{129,130},{2,1},{130,131},{3,2},{131,132},{4... | collective-permute-start | bytes 786440 | tf_op jit(solution)/shard_map/ppermute | solution.py:28
  146.8 3.4 %shard_map.101 = (bf16[64,2048]{1,0:T(8,128)(2,1)S(1)}, bf16[64,2048]{1,0:T(8,128)(2,1)S(1)}) custom-call(s32[3]{0:T(128)S(1)} %pad_add_fusion.flip_ref, bf16[64,2048]{1,0:T(8,128)(2,1)S(1)} %collective-permute-done.16.refs_0_, bf16[64,2048]{1,0:T(8,128)(2,1)S(1)} %collective-permute-done.17.refs_1_, bf16[128,1024]{1,0:T(8,128)(2,1)S(1)} %get-tuple-element.54.refs_2_, ...), custom_call_target="tpu_custom_call" | custom-call | flops 268435456 | bytes 1048576 | tf_op jit(solution)/shard_map/pallas_call | solution.py:217
  150.3 0.9 collective-permute-done.15
  151.5 3.8 %collective-permute-start.21 = (bf16[64,2048]{1,0:T(8,128)(2,1)S(1)}, bf16[64,2048]{1,0:T(8,128)(2,1)S(1)}, u32[]{:S(2)}, u32[]{:S(2)}) collective-permute-start(bf16[64,2048]{1,0:T(8,128)(2,1)S(1)} %add_convert_fusion.2), channel_id=1, source_target_pairs={{0,7},{128,129},{1,0},{129,130},{2,1},{130,131},{3,2},{131,132},{4... | collective-permute-start | bytes 786440 | tf_op jit(solution)/shard_map/ppermute | solution.py:28
  155.3 3.8 %collective-permute-done.18 = bf16[64,2048]{1,0:T(8,128)(2,1)S(1)} collective-permute-done((bf16[64,2048]{1,0:T(8,128)(2,1)S(1)}, bf16[64,2048]{1,0:T(8,128)(2,1)S(1)}, u32[]{:S(2)}, u32[]{:S(2)}) %collective-permute-start.18) | collective-permute-done | bytes 262176 | tf_op jit(solution)/shard_map/ppermute | solution.py:28
  159.3 3.7 %collective-permute-start.22 = (bf16[64,2048]{1,0:T(8,128)(2,1)S(1)}, bf16[64,2048]{1,0:T(8,128)(2,1)S(1)}, u32[]{:S(2)}, u32[]{:S(2)}) collective-permute-start(bf16[64,2048]{1,0:T(8,128)(2,1)S(1)} %add_convert_fusion.1), channel_id=1, source_target_pairs={{0,7},{128,129},{1,0},{129,130},{2,1},{130,131},{3,2},{131,132},{4... | collective-permute-start | bytes 786440 | tf_op jit(solution)/shard_map/ppermute | solution.py:28
  163.0 3.8 %collective-permute-done.19 = bf16[64,2048]{1,0:T(8,128)(2,1)S(1)} collective-permute-done((bf16[64,2048]{1,0:T(8,128)(2,1)S(1)}, bf16[64,2048]{1,0:T(8,128)(2,1)S(1)}, u32[]{:S(2)}, u32[]{:S(2)}) %collective-permute-start.19) | collective-permute-done | bytes 262176 | tf_op jit(solution)/shard_map/ppermute | solution.py:28
  167.2 11.8 %all_to_all.23 = bf16[16,64,128]{2,1,0:T(8,128)(2,1)S(1)} all-to-all(bf16[16,64,128]{2,1,0:T(8,128)(2,1)S(1)} %reshape.44), channel_id=1, replica_groups={{0,8,16,24,32,40,48,56,64,72,80,88,96,104,112,120},{1,9,17,25,33,41,49,..., dimensions={0} | all-to-all | bytes 524288 | tf_op jit(solution)/shard_map/all_to_all | solution.py:37
  179.1 1.6 shard_map.102
  (57 shorter events, 3.4 us)
Async XLA Ops:
  1.3 1.0 copy-start.5
  2.3 0.7 copy-start.7
  3.0 36.0 %copy-start.9 = (bf16[2,128,1024]{2,1,0:T(8,128)(2,1)S(1)}, bf16[2,128,1024]{2,1,0:T(8,128)(2,1)}, u32[]{:S(2)}) copy-start(bf16[2,128,1024]{2,1,0:T(8,128)(2,1)} %param.13) | copy-start | bytes 1572868
  33.4 15.9 %collective-permute-start.1 = (bf16[128,2048]{1,0:T(8,128)(2,1)S(1)}, bf16[128,2048]{1,0:T(8,128)(2,1)S(1)}, u32[]{:S(2)}, u32[]{:S(2)}) collective-permute-start(bf16[128,2048]{1,0:T(8,128)(2,1)S(1)} %reshape.39.refs_0_), channel_id=1, source_target_pairs={{0,1},{128,135},{1,2},{129,128},{2,3},{130,129},{3,4},{131,130},{4... | collective-permute-start | bytes 1572872 | tf_op jit(solution)/shard_map/ppermute | solution.py:28
  39.0 13.7 %collective-permute-start.2 = (bf16[128,2048]{1,0:T(8,128)(2,1)S(1)}, bf16[128,2048]{1,0:T(8,128)(2,1)S(1)}, u32[]{:S(2)}, u32[]{:S(2)}) collective-permute-start(bf16[128,2048]{1,0:T(8,128)(2,1)S(1)} %reshape.39.refs_0_), channel_id=1, source_target_pairs={{0,7},{128,129},{1,0},{129,130},{2,1},{130,131},{3,2},{131,132},{4... | collective-permute-start | bytes 1572872 | tf_op jit(solution)/shard_map/ppermute | solution.py:28
  39.2 2.2 %copy-start = (bf16[1,2048,1024]{2,1,0:T(8,128)(2,1)S(1)}, bf16[1,2048,1024]{2,1,0:T(8,128)(2,1)}, u32[]{:S(2)}) copy-start(bf16[1,2048,1024]{2,1,0:T(8,128)(2,1)} %param.11) | copy-start | bytes 12582916
  41.4 2.2 %copy-start.3 = (bf16[1,1024,2048]{2,1,0:T(8,128)(2,1)S(1)}, bf16[1,1024,2048]{2,1,0:T(8,128)(2,1)}, u32[]{:S(2)}) copy-start(bf16[1,1024,2048]{2,1,0:T(8,128)(2,1)} %param.12) | copy-start | bytes 12582916
  43.6 9.3 %copy-start.1 = (bf16[1,2048,1024]{2,1,0:T(8,128)(2,1)S(1)}, bf16[1,2048,1024]{2,1,0:T(8,128)(2,1)}, u32[]{:S(2)}) copy-start(bf16[1,2048,1024]{2,1,0:T(8,128)(2,1)} %param.11) | copy-start | bytes 12582916
  45.5 10.3 %collective-permute-start = (bf16[64,2048]{1,0:T(8,128)(2,1)S(1)}, bf16[64,2048]{1,0:T(8,128)(2,1)S(1)}, u32[]{:S(2)}, u32[]{:S(2)}) collective-permute-start(bf16[64,2048]{1,0:T(8,128)(2,1)S(1)} %get-tuple-element.36), channel_id=1, source_target_pairs={{0,1},{128,135},{1,2},{129,128},{2,3},{130,129},{3,4},{131,130},{4... | collective-permute-start | bytes 786440 | tf_op jit(solution)/shard_map/ppermute | solution.py:28
  49.3 10.4 %collective-permute-start.4 = (bf16[64,2048]{1,0:T(8,128)(2,1)S(1)}, bf16[64,2048]{1,0:T(8,128)(2,1)S(1)}, u32[]{:S(2)}, u32[]{:S(2)}) collective-permute-start(bf16[64,2048]{1,0:T(8,128)(2,1)S(1)} %slice_select_fusion.3), channel_id=1, source_target_pairs={{0,1},{128,135},{1,2},{129,128},{2,3},{130,129},{3,4},{131,130},{4... | collective-permute-start | bytes 786440 | tf_op jit(solution)/shard_map/ppermute | solution.py:28
  52.8 8.7 %collective-permute-start.5 = (bf16[64,2048]{1,0:T(8,128)(2,1)S(1)}, bf16[64,2048]{1,0:T(8,128)(2,1)S(1)}, u32[]{:S(2)}, u32[]{:S(2)}) collective-permute-start(bf16[64,2048]{1,0:T(8,128)(2,1)S(1)} %slice_select_fusion.2), channel_id=1, source_target_pairs={{0,7},{128,129},{1,0},{129,130},{2,1},{130,131},{3,2},{131,132},{4... | collective-permute-start | bytes 786440 | tf_op jit(solution)/shard_map/ppermute | solution.py:28
  55.9 8.5 %collective-permute-start.3 = (bf16[64,2048]{1,0:T(8,128)(2,1)S(1)}, bf16[64,2048]{1,0:T(8,128)(2,1)S(1)}, u32[]{:S(2)}, u32[]{:S(2)}) collective-permute-start(bf16[64,2048]{1,0:T(8,128)(2,1)S(1)} %add_convert_fusion.11), channel_id=1, source_target_pairs={{0,1},{128,135},{1,2},{129,128},{2,3},{130,129},{3,4},{131,130},{4... | collective-permute-start | bytes 786440 | tf_op jit(solution)/shard_map/ppermute | solution.py:28
  58.0 8.2 %collective-permute-start.8 = (bf16[64,2048]{1,0:T(8,128)(2,1)S(1)}, bf16[64,2048]{1,0:T(8,128)(2,1)S(1)}, u32[]{:S(2)}, u32[]{:S(2)}) collective-permute-start(bf16[64,2048]{1,0:T(8,128)(2,1)S(1)} %get-tuple-element.41), channel_id=1, source_target_pairs={{0,7},{128,129},{1,0},{129,130},{2,1},{130,131},{3,2},{131,132},{4... | collective-permute-start | bytes 786440 | tf_op jit(solution)/shard_map/ppermute | solution.py:28
  63.4 30.8 %copy-start.6 = (bf16[1,128,2048]{2,1,0:T(8,128)(2,1)S(1)}, bf16[1,128,2048]{2,1,0:T(8,128)(2,1)}, u32[]{:S(2)}) copy-start(bf16[1,128,2048]{2,1,0:T(8,128)(2,1)} %param.7) | copy-start | bytes 1572868
  63.4 30.8 %copy-start.8 = (f32[1,128,2]{1,2,0:T(2,128)S(1)}, f32[1,128,2]{1,2,0:T(2,128)}, u32[]{:S(2)}) copy-start(f32[1,128,2]{1,2,0:T(2,128)} %param.9) | copy-start | bytes 3076
  64.5 8.2 %collective-permute-start.6 = (bf16[64,2048]{1,0:T(8,128)(2,1)S(1)}, bf16[64,2048]{1,0:T(8,128)(2,1)S(1)}, u32[]{:S(2)}, u32[]{:S(2)}) collective-permute-start(bf16[64,2048]{1,0:T(8,128)(2,1)S(1)} %add_convert_fusion.10), channel_id=1, source_target_pairs={{0,1},{128,135},{1,2},{129,128},{2,3},{130,129},{3,4},{131,130},{4... | collective-permute-start | bytes 786440 | tf_op jit(solution)/shard_map/ppermute | solution.py:28
  66.2 9.1 %collective-permute-start.9 = (bf16[64,2048]{1,0:T(8,128)(2,1)S(1)}, bf16[64,2048]{1,0:T(8,128)(2,1)S(1)}, u32[]{:S(2)}, u32[]{:S(2)}) collective-permute-start(bf16[64,2048]{1,0:T(8,128)(2,1)S(1)} %add_convert_fusion.8), channel_id=1, source_target_pairs={{0,7},{128,129},{1,0},{129,130},{2,1},{130,131},{3,2},{131,132},{4... | collective-permute-start | bytes 786440 | tf_op jit(solution)/shard_map/ppermute | solution.py:28
  72.8 7.7 %collective-permute-start.7 = (bf16[64,2048]{1,0:T(8,128)(2,1)S(1)}, bf16[64,2048]{1,0:T(8,128)(2,1)S(1)}, u32[]{:S(2)}, u32[]{:S(2)}) collective-permute-start(bf16[64,2048]{1,0:T(8,128)(2,1)S(1)} %add_convert_fusion.9), channel_id=1, source_target_pairs={{0,1},{128,135},{1,2},{129,128},{2,3},{130,129},{3,4},{131,130},{4... | collective-permute-start | bytes 786440 | tf_op jit(solution)/shard_map/ppermute | solution.py:28
  75.4 6.5 %collective-permute-start.10 = (bf16[64,2048]{1,0:T(8,128)(2,1)S(1)}, bf16[64,2048]{1,0:T(8,128)(2,1)S(1)}, u32[]{:S(2)}, u32[]{:S(2)}) collective-permute-start(bf16[64,2048]{1,0:T(8,128)(2,1)S(1)} %add_convert_fusion.7), channel_id=1, source_target_pairs={{0,7},{128,129},{1,0},{129,130},{2,1},{130,131},{3,2},{131,132},{4... | collective-permute-start | bytes 786440 | tf_op jit(solution)/shard_map/ppermute | solution.py:28
  77.8 16.4 %collective-permute-start.11 = (bf16[128,1024]{1,0:T(8,128)(2,1)S(1)}, bf16[128,1024]{1,0:T(8,128)(2,1)S(1)}, u32[]{:S(2)}, u32[]{:S(2)}) collective-permute-start(bf16[128,1024]{1,0:T(8,128)(2,1)S(1)} %get-tuple-element.45), channel_id=1, source_target_pairs={{0,128},{128,0},{1,129},{129,1},{2,130},{130,2},{3,131},{131,3},{4... | collective-permute-start | bytes 786440 | tf_op jit(solution)/shard_map/ppermute | solution.py:278
  118.3 15.6 %collective-permute-start.13 = (bf16[128,2048]{1,0:T(8,128)(2,1)S(1)}, bf16[128,2048]{1,0:T(8,128)(2,1)S(1)}, u32[]{:S(2)}, u32[]{:S(2)}) collective-permute-start(bf16[128,2048]{1,0:T(8,128)(2,1)S(1)} %reshape.43.refs_0_), channel_id=1, source_target_pairs={{0,1},{128,135},{1,2},{129,128},{2,3},{130,129},{3,4},{131,130},{4... | collective-permute-start | bytes 1572872 | tf_op jit(solution)/shard_map/ppermute | solution.py:28
  118.4 18.7 %collective-permute-start.14 = (bf16[128,2048]{1,0:T(8,128)(2,1)S(1)}, bf16[128,2048]{1,0:T(8,128)(2,1)S(1)}, u32[]{:S(2)}, u32[]{:S(2)}) collective-permute-start(bf16[128,2048]{1,0:T(8,128)(2,1)S(1)} %reshape.43.refs_0_), channel_id=1, source_target_pairs={{0,7},{128,129},{1,0},{129,130},{2,1},{130,131},{3,2},{131,132},{4... | collective-permute-start | bytes 1572872 | tf_op jit(solution)/shard_map/ppermute | solution.py:28
  124.1 2.2 %copy-start.2 = (bf16[1,2048,1024]{2,1,0:T(8,128)(2,1)S(1)}, bf16[1,2048,1024]{2,1,0:T(8,128)(2,1)}, u32[]{:S(2)}) copy-start(bf16[1,2048,1024]{2,1,0:T(8,128)(2,1)} %param.11) | copy-start | bytes 12582916
  126.3 2.2 %copy-start.4 = (bf16[1,1024,2048]{2,1,0:T(8,128)(2,1)S(1)}, bf16[1,1024,2048]{2,1,0:T(8,128)(2,1)}, u32[]{:S(2)}) copy-start(bf16[1,1024,2048]{2,1,0:T(8,128)(2,1)} %param.12) | copy-start | bytes 12582916
  131.9 11.5 %collective-permute-start.12 = (bf16[64,2048]{1,0:T(8,128)(2,1)S(1)}, bf16[64,2048]{1,0:T(8,128)(2,1)S(1)}, u32[]{:S(2)}, u32[]{:S(2)}) collective-permute-start(bf16[64,2048]{1,0:T(8,128)(2,1)S(1)} %get-tuple-element.51), channel_id=1, source_target_pairs={{0,1},{128,135},{1,2},{129,128},{2,3},{130,129},{3,4},{131,130},{4... | collective-permute-start | bytes 786440 | tf_op jit(solution)/shard_map/ppermute | solution.py:28
  134.0 12.8 %collective-permute-start.16 = (bf16[64,2048]{1,0:T(8,128)(2,1)S(1)}, bf16[64,2048]{1,0:T(8,128)(2,1)S(1)}, u32[]{:S(2)}, u32[]{:S(2)}) collective-permute-start(bf16[64,2048]{1,0:T(8,128)(2,1)S(1)} %slice_select_fusion.1), channel_id=1, source_target_pairs={{0,1},{128,135},{1,2},{129,128},{2,3},{130,129},{3,4},{131,130},{4... | collective-permute-start | bytes 786440 | tf_op jit(solution)/shard_map/ppermute | solution.py:28
  137.2 9.7 %collective-permute-start.17 = (bf16[64,2048]{1,0:T(8,128)(2,1)S(1)}, bf16[64,2048]{1,0:T(8,128)(2,1)S(1)}, u32[]{:S(2)}, u32[]{:S(2)}) collective-permute-start(bf16[64,2048]{1,0:T(8,128)(2,1)S(1)} %slice_select_fusion), channel_id=1, source_target_pairs={{0,7},{128,129},{1,0},{129,130},{2,1},{130,131},{3,2},{131,132},{4... | collective-permute-start | bytes 786440 | tf_op jit(solution)/shard_map/ppermute | solution.py:28
  143.5 7.7 %collective-permute-start.15 = (bf16[64,2048]{1,0:T(8,128)(2,1)S(1)}, bf16[64,2048]{1,0:T(8,128)(2,1)S(1)}, u32[]{:S(2)}, u32[]{:S(2)}) collective-permute-start(bf16[64,2048]{1,0:T(8,128)(2,1)S(1)} %add_convert_fusion.5), channel_id=1, source_target_pairs={{0,1},{128,135},{1,2},{129,128},{2,3},{130,129},{3,4},{131,130},{4... | collective-permute-start | bytes 786440 | tf_op jit(solution)/shard_map/ppermute | solution.py:28
  143.6 7.9 %collective-permute-start.20 = (bf16[64,2048]{1,0:T(8,128)(2,1)S(1)}, bf16[64,2048]{1,0:T(8,128)(2,1)S(1)}, u32[]{:S(2)}, u32[]{:S(2)}) collective-permute-start(bf16[64,2048]{1,0:T(8,128)(2,1)S(1)} %get-tuple-element.57), channel_id=1, source_target_pairs={{0,7},{128,129},{1,0},{129,130},{2,1},{130,131},{3,2},{131,132},{4... | collective-permute-start | bytes 786440 | tf_op jit(solution)/shard_map/ppermute | solution.py:28
  151.2 7.8 %collective-permute-start.18 = (bf16[64,2048]{1,0:T(8,128)(2,1)S(1)}, bf16[64,2048]{1,0:T(8,128)(2,1)S(1)}, u32[]{:S(2)}, u32[]{:S(2)}) collective-permute-start(bf16[64,2048]{1,0:T(8,128)(2,1)S(1)} %add_convert_fusion.4), channel_id=1, source_target_pairs={{0,1},{128,135},{1,2},{129,128},{2,3},{130,129},{3,4},{131,130},{4... | collective-permute-start | bytes 786440 | tf_op jit(solution)/shard_map/ppermute | solution.py:28
  151.5 7.7 %collective-permute-start.21 = (bf16[64,2048]{1,0:T(8,128)(2,1)S(1)}, bf16[64,2048]{1,0:T(8,128)(2,1)S(1)}, u32[]{:S(2)}, u32[]{:S(2)}) collective-permute-start(bf16[64,2048]{1,0:T(8,128)(2,1)S(1)} %add_convert_fusion.2), channel_id=1, source_target_pairs={{0,7},{128,129},{1,0},{129,130},{2,1},{130,131},{3,2},{131,132},{4... | collective-permute-start | bytes 786440 | tf_op jit(solution)/shard_map/ppermute | solution.py:28
  159.2 7.7 %collective-permute-start.19 = (bf16[64,2048]{1,0:T(8,128)(2,1)S(1)}, bf16[64,2048]{1,0:T(8,128)(2,1)S(1)}, u32[]{:S(2)}, u32[]{:S(2)}) collective-permute-start(bf16[64,2048]{1,0:T(8,128)(2,1)S(1)} %add_convert_fusion.3), channel_id=1, source_target_pairs={{0,1},{128,135},{1,2},{129,128},{2,3},{130,129},{3,4},{131,130},{4... | collective-permute-start | bytes 786440 | tf_op jit(solution)/shard_map/ppermute | solution.py:28
  159.3 7.6 %collective-permute-start.22 = (bf16[64,2048]{1,0:T(8,128)(2,1)S(1)}, bf16[64,2048]{1,0:T(8,128)(2,1)S(1)}, u32[]{:S(2)}, u32[]{:S(2)}) collective-permute-start(bf16[64,2048]{1,0:T(8,128)(2,1)S(1)} %add_convert_fusion.1), channel_id=1, source_target_pairs={{0,7},{128,129},{1,0},{129,130},{2,1},{130,131},{3,2},{131,132},{4... | collective-permute-start | bytes 786440 | tf_op jit(solution)/shard_map/ppermute | solution.py:28
